TPU v7x, 128 devices: a whole 4x4x4 slice. The times are simulated.
128 devices in a mesh: pair: 8 (over y, core), coup: 16 (over z, x).
Axes of the slice: x: 4, y: 4, z: 4, core: 2. Of those that a mesh axis runs over, the one named last changes fastest.
Arguments:
- amplitudes: bfloat16 [1024, 256, 256], P(('pair', 'coup')), may hold values from -6 to 6
- integrals: bfloat16 [1024, 256, 256], P(('pair', 'coup')), may hold values from -6 to 6
- pno_energy: float32 [1024, 256], P(('pair', 'coup')), may hold values from 0.2 to 1.5
- occ_energy: float32 [32], replicated, may hold values from -0.8 to -0.2
- occ_fock: float32 [32, 32], replicated, may hold values from -2 to 2
- row_intersection: bfloat16 [1024, 6, 256, 256], P(('pair', 'coup')), may hold values from -0.375 to 0.375
- column_intersection: bfloat16 [1024, 6, 256, 256], P(('pair', 'coup')), may hold values from -0.375 to 0.375
- row_peer: int32 [1024, 6, 1], P(('pair', 'coup')), may hold values from 0 to 15; in each aligned block of 48 rows (0 to 47, 48 to 95, ..., all dimensions but the last counted through in order) at most 4 rows name the same one
- row_offset: int32 [1024, 6], P(('pair', 'coup')), may hold values from 0 to 1
- column_partner: int32 [1024, 6], P(('pair', 'coup')), may hold values from 0 to 31
- pno_count: int32 [1024], P(('pair', 'coup')), may hold values from 128 to 256
Outputs:
- residual: bfloat16 [1024, 256, 256], P(('pair', 'coup'))
- new_amplitudes: bfloat16 [1024, 256, 256], P(('pair', 'coup'))
Inputs may be any that keep to these rules, and one draw needn't show every extreme that they name: `row_peer`: among the 48 rows of one device, at most 4 name the same value, a bound that some block reaches.
All inputs are finite; a program needn't handle non-finite values.
Results may differ from a plain program's by a relative error of at most 0.009.
Values may be sent and summed in bfloat16 or wider, within the bound.
A program may use at most 128 MiB of HBM per device.

v0:
```python
import jax
import jax.numpy as jnp
from jax import lax
from jax.sharding import PartitionSpec as P

JB = 2


def pick_blocks(wanted, carry, piece):
    count = piece.shape[0]
    inside = (wanted >= 0) & (wanted < count)
    picked = jnp.take(piece, jnp.clip(wanted, 0, count - 1), axis=0)
    return jnp.where(inside[:, None, None], picked, carry)


def sandwich(shared_orbitals, block_list):
    central_product = jnp.einsum(
        "wxl,wlh->wxh", shared_orbitals, block_list, preferred_element_type=jnp.float32
    ).astype(jnp.bfloat16)
    return jnp.einsum(
        "nfe,nwe->nfw", central_product, shared_orbitals, preferred_element_type=jnp.float32
    )


def on_device(
    amplitudes,
    integrals,
    pno_energy,
    occ_energy,
    occ_fock,
    row_intersection,
    column_intersection,
    row_peer,
    row_offset,
    column_partner,
    pno_count,
):
    pairs_here, width, _ = amplitudes.shape
    links = row_offset.shape[1]
    first_block = pairs_here // JB
    nocc = occ_energy.shape[0]
    my_row = lax.axis_index("pair")
    own_column = lax.axis_index("coup")
    local = jnp.arange(pairs_here, dtype=jnp.int32)
    first = my_row * first_block + local // JB
    second = own_column * JB + local % JB
    peers = row_peer[:, :, 0]
    partner_k = peers * JB + row_offset
    source_local = (local // JB)[:, None] * JB + row_offset
    tasks = pairs_here * links
    flat_peers = peers.reshape(tasks)
    flat_source = source_local.reshape(tasks)
    empty = jnp.zeros((tasks, width, width), jnp.bfloat16)
    row_wanted = flat_peers * pairs_here + flat_source
    row_blocks = pick_blocks(
        row_wanted, empty, lax.all_gather(amplitudes, "coup", axis=0, tiled=True)
    )
    column_wanted = (
        column_partner // first_block * pairs_here
        + column_partner % first_block * JB
        + (local % JB)[:, None]
    ).reshape(tasks)
    column_blocks = pick_blocks(
        column_wanted, empty, lax.all_gather(amplitudes, "pair", axis=0, tiled=True)
    )
    orbitals = jnp.arange(nocc, dtype=jnp.int32)
    row_match = (partner_k[:, :, None, None] == orbitals[None, None, :, None]) & (
        second[:, None, None, None] == orbitals[None, None, None, :]
    )
    row_fock = jnp.sum(jnp.where(row_match, occ_fock[None, None], 0.0), axis=(2, 3))
    column_match = (first[:, None, None, None] == orbitals[None, None, :, None]) & (
        column_partner[:, :, None, None] == orbitals[None, None, None, :]
    )
    column_fock_matrix = jnp.sum(jnp.where(column_match, occ_fock[None, None], 0.0), axis=(2, 3))
    row_terms = sandwich(row_intersection.reshape(tasks, width, width), row_blocks).reshape(
        pairs_here, links, width, width
    )
    column_terms = sandwich(
        column_intersection.reshape(tasks, width, width), column_blocks
    ).reshape(pairs_here, links, width, width)
    row_term = jnp.sum(row_fock[:, :, None, None] * row_terms, axis=1)
    column_term = jnp.sum(column_fock_matrix[:, :, None, None] * column_terms, axis=1)
    first_energy = jnp.sum(
        jnp.where(first[:, None] == orbitals[None, :], occ_energy[None, :], 0.0), axis=1
    )
    second_energy = jnp.sum(
        jnp.where(second[:, None] == orbitals[None, :], occ_energy[None, :], 0.0), axis=1
    )
    energy_denominator = (
        pno_energy[:, :, None]
        + pno_energy[:, None, :]
        - (first_energy + second_energy)[:, None, None]
    )
    present = (jnp.arange(width, dtype=jnp.int32)[None, :] < pno_count[:, None]).astype(jnp.float32)
    mask = present[:, :, None] * present[:, None, :]
    current = amplitudes.astype(jnp.float32)
    full = integrals.astype(jnp.float32) + energy_denominator * current - row_term - column_term
    residual = (mask * full).astype(jnp.bfloat16)
    new_amplitudes = (mask * (current - full / energy_denominator)).astype(jnp.bfloat16)
    return (residual, new_amplitudes)


def solution(mesh):
    return jax.shard_map(
        on_device,
        mesh=mesh,
        in_specs=(
            P(("pair", "coup"), None, None),
            P(("pair", "coup"), None, None),
            P(("pair", "coup"), None),
            P(),
            P(),
            P(("pair", "coup"), None, None, None),
            P(("pair", "coup"), None, None, None),
            P(("pair", "coup"), None, None),
            P(("pair", "coup"), None),
            P(("pair", "coup"), None),
            P(("pair", "coup")),
        ),
        out_specs=(P(("pair", "coup"), None, None), P(("pair", "coup"), None, None)),
        check_vma=False,
    )
```

profile of v0, /device:TPU:0, one launch (start us, length us, event | category | flops | bytes accessed | tf_op | source)
XLA Modules:
  0.0 215.4 jit_solution(10636385153252880694)
XLA Ops:
  7.2 0.0 all-gather.5.cloned.1.call-start
  7.2 0.7 all-gather.5.cloned.1.call-update
  7.9 0.0 all-gather.3.cloned.1.call-start
  7.9 0.7 all-gather.3.cloned.1.call-update
  8.7 0.8 copy.26
  9.4 0.8 broadcast_add_fusion
  10.2 0.1 reshape.290
  10.3 0.1 reshape.291
  10.3 0.7 broadcast_multiply_fusion
  11.0 0.1 copy.27
  11.1 0.1 mul.103
  11.2 0.1 mul.105
  11.3 0.8 compare_and_fusion
  12.0 0.1 min.32
  12.1 0.1 min.30
  12.2 0.1 and.140
  12.3 0.9 select_reduce_fusion.2
  13.2 0.1 iota_compare_fusion.3
  13.3 0.1 iota_compare_fusion.4
  13.4 0.8 iota_compare_fusion
  14.2 1.3 select_reduce_fusion.1
  15.5 0.7 fusion.35
  16.2 45.7 %all-gather.5.cloned.1.call-done = bf16[64,256,256]{2,1,0:T(8,128)(2,1)} async-done(((bf16[8,256,256]{2,1,0:T(8,128)(2,1)}), bf16[64,256,256]{2,1,0:T(8,128)(2,1)}) %all-gather.5.cloned.1.call-update) | async-done | bytes 8388624 | tf_op jit(solution)/shard_map/all_gather | solution.py:64
  61.9 8.3 %gather_fusion.1 = bf16[48,256,256]{2,1,0:T(8,128)(2,1)} fusion(bf16[64,256,256]{2,1,0:T(8,128)(2,1)} %all-gather.5.cloned.1.call-done, s32[1024]{0:T(1024)S(1)} %pad_clamp_fusion), kind=kCustom, calls=%fused_computation.1 | custom fusion | bytes 12583104 | tf_op jit(solution)/shard_map/jit(_take)/gather | solution.py:12
  70.3 13.1 %fusion = f32[48,256,256]{2,1,0:T(8,128)} fusion(bf16[48,256,256]{2,1,0:T(8,128)(2,1)} %bitcast.20, bf16[48,256,256]{2,1,0:T(8,128)(2,1)} %gather_fusion.1, pred[48]{0:T(512)(128)(4,1)S(1)} %compare_and_fusion.1, pred[48]{0:T(512)(128)(4,1)S(1)} %and.140), kind=kOutput, calls=%fused_computation.4 | convolution fusion | flops 3230662656 | bytes 25165920 | tf_op jit(solution)/shard_map/nfe,nwe->nfw/dot_general | solution.py:20
  83.4 6.6 %multiply_reduce_fusion = f32[8,256,256]{2,1,0:T(8,128)S(1)} fusion(f32[8,6,256,256]{3,2,1,0:T(8,128)} %bitcast.19, f32[8,6]{1,0:T(8,128)S(1)} %get-tuple-element.3), kind=kLoop, calls=%fused_computation.2 | loop fusion | flops 5767168 | bytes 14680256 | tf_op jit(solution)/shard_map/reduce_sum | solution.py:82
  90.0 85.8 %all-gather.3.cloned.1.call-done = bf16[128,256,256]{2,1,0:T(8,128)(2,1)} async-done(((bf16[8,256,256]{2,1,0:T(8,128)(2,1)}), bf16[128,256,256]{2,1,0:T(8,128)(2,1)}) %all-gather.3.cloned.1.call-update) | async-done | bytes 16777232 | tf_op jit(solution)/shard_map/all_gather | solution.py:56
  175.7 10.7 %gather_fusion = bf16[48,256,256]{2,1,0:T(8,128)(2,1)} fusion(bf16[128,256,256]{2,1,0:T(8,128)(2,1)} %all-gather.3.cloned.1.call-done, s32[1024]{0:T(1024)S(1)} %pad_clamp_fusion.1), kind=kCustom, calls=%fused_computation | custom fusion | bytes 12583104 | tf_op jit(solution)/shard_map/jit(_take)/gather | solution.py:12
  186.5 13.2 %fusion.5 = f32[48,256,256]{2,1,0:T(8,128)} fusion(bf16[48,256,256]{2,1,0:T(8,128)(2,1)} %bitcast.21, bf16[48,256,256]{2,1,0:T(8,128)(2,1)} %gather_fusion, pred[48]{0:T(512)(128)(4,1)S(1)} %get-tuple-element.13, pred[48]{0:T(512)(128)(4,1)S(1)} %get-tuple-element.12), kind=kOutput, calls=%fused_computation.9 | convolution fusion | flops 3230662656 | bytes 25165920 | tf_op jit(solution)/shard_map/nfe,nwe->nfw/dot_general | solution.py:20
  199.7 0.0 copy-start
  199.7 0.0 copy-start.1
  199.7 0.0 copy-start.2
  199.7 6.5 %multiply_reduce_fusion.1 = f32[8,256,256]{2,1,0:T(8,128)S(1)} fusion(f32[8,6,256,256]{3,2,1,0:T(8,128)} %bitcast.18, f32[8,6]{1,0:T(8,128)S(1)} %get-tuple-element.2), kind=kLoop, calls=%fused_computation.3 | loop fusion | flops 5767168 | bytes 14680256 | tf_op jit(solution)/shard_map/reduce_sum | solution.py:81
  206.1 0.0 copy-done
  206.2 0.0 copy-done.1
  206.2 0.0 copy-done.2
  206.2 2.3 %fusion.34 = (bf16[8,256,256]{2,1,0:T(8,128)(2,1)}, bf16[8,256,256]{2,1,0:T(8,128)(2,1)}) fusion(bf16[8,256,256]{2,1,0:T(8,128)(2,1)S(1)} %copy-done, f32[8]{0:T(128)S(1)} %add.173, f32[8,256]{1,0:T(8,128)S(1)} %copy-done.2, f32[8,256]{1,0:T(8,128)S(1)} %fusion.35, f32[8,256,256]{2,1,0:T(8,128)S(1)} %multiply_reduce_fusion, ...), kind=kLoop, calls=%fused_computation.30 | loop fusion | flops 7864320 | bytes 8405024 | tf_op jit(solution)/shard_map/convert_element_type | solution.py:99
  (11 shorter events, 0.1 us)
Async XLA Ops:
  7.2 54.8 %all-gather.5.cloned.1.call-start = ((), (), s32[]{:S(2)}) async-start(), calls=%async_computation.1 | async-start | bytes 9437184 | tf_op jit(solution)/shard_map/all_gather | solution.py:64
  7.9 167.9 %all-gather.3.cloned.1.call-start = ((), (), s32[]{:S(2)}) async-start(), calls=%async_computation | async-start | bytes 17825792 | tf_op jit(solution)/shard_map/all_gather | solution.py:56
  199.7 6.5 %copy-start = (bf16[8,256,256]{2,1,0:T(8,128)(2,1)S(1)}, bf16[8,256,256]{2,1,0:T(8,128)(2,1)}, u32[]{:S(2)}) copy-start(bf16[8,256,256]{2,1,0:T(8,128)(2,1)} %param.11) | copy-start | bytes 3145732
  199.7 6.5 %copy-start.1 = (bf16[8,256,256]{2,1,0:T(8,128)(2,1)S(1)}, bf16[8,256,256]{2,1,0:T(8,128)(2,1)}, u32[]{:S(2)}) copy-start(bf16[8,256,256]{2,1,0:T(8,128)(2,1)} %param.12) | copy-start | bytes 3145732
  199.7 6.5 %copy-start.2 = (f32[8,256]{1,0:T(8,128)S(1)}, f32[8,256]{1,0:T(8,128)}, u32[]{:S(2)}) copy-start(f32[8,256]{1,0:T(8,128)} %param.13) | copy-start | bytes 24580
Sparse Core Ops, SparseCore 0:
  9.7 52.1 all-gather.4
  64.1 111.6 all-gather.2
where the time goes:
time: 217 us; the launch traced here: 215 us
  waiting for transfers between devices  133 us (61%)
  matrix products  26.3 us (12%)
  other arithmetic  21.5 us (10%)
  local copies, waits for them, and re-layouts  20.5 us (9%)
  between operations  14.1 us (6%)
    all_gather x1, waiting for transfers between devices, on_device(): lax.all_gather(amplitudes, 'coup', axis=0, tiled=True)  85.8 us
    all_gather x1, waiting for transfers between devices, on_device(): lax.all_gather(amplitudes, 'pair', axis=0, tiled=True)  45.7 us
    dot_general x2, matrix products, sandwich(): jnp.einsum('nfe,nwe->nfw', central_product, shared_orbitals, preferred_el...  26.3 us
    gather x2, local copies, waits for them, and re-layouts, pick_blocks(): picked = jnp.take(piece, jnp.clip(wanted, 0, count - 1), axis=0)  19.1 us
    reduce_sum x1, other arithmetic, on_device(): jnp.sum(column_fock_matrix[:, :, None, None] * column_terms, axis=1)  6.58 us
    reduce_sum x1, other arithmetic, on_device(): row_term = jnp.sum(row_fock[:, :, None, None] * row_terms, axis=1)  6.47 us
  transfers between devices with their start and end apart: 2, of which 2 were waited for; matrix products, arithmetic and copies ran while one was open for 17% of the time, Pallas kernels for 0%

commit v1 on v0

v1 whole, which is shorter than its diff:
```python
import functools

import jax
import jax.numpy as jnp
from jax import lax
from jax.experimental import pallas as pl
from jax.experimental.pallas import tpu as pltpu
from jax.sharding import PartitionSpec as P

MESH = pl.DeviceIdType.MESH
V = 256
HALF = 128
BLOCKS = 8
LINKS = 6
TASKS = BLOCKS * LINKS
CAP = 4
SIDE = 4
N_COUP = 16

TREE = {
    (0, 1): (0, 0), (3, 0): (0, 0), (1, 1): (0, 1), (3, 3): (3, 0), (1, 2): (1, 1),
    (0, 3): (0, 0), (1, 0): (0, 0), (0, 2): (0, 1), (2, 0): (3, 0), (2, 1): (1, 1), (2, 3): (3, 3),
    (3, 1): (0, 1), (3, 2): (3, 3), (1, 3): (1, 2), (2, 2): (1, 2),
}
ROOT = (0, 0)
ORDER = [
    (0, (0, 1)), (1, (0, 1)), (0, (3, 0)), (1, (3, 0)),
    (0, (0, 3)), (0, (1, 0)), (1, (0, 3)), (1, (1, 0)),
    (0, (1, 1)), (1, (1, 1)), (0, (3, 3)), (1, (3, 3)),
    (0, (0, 2)), (0, (2, 0)), (1, (0, 2)), (1, (2, 0)),
    (0, (1, 2)), (1, (1, 2)), (0, (2, 1)), (0, (2, 3)),
    (0, (3, 1)), (1, (2, 1)),
    (0, (3, 2)), (1, (2, 3)), (1, (3, 1)), (1, (3, 2)),
    (0, (1, 3)), (0, (2, 2)), (1, (1, 3)), (1, (2, 2)),
]
INNER = [n for n in TREE if n in TREE.values()]
LEAVES = [n for n in TREE if n not in TREE.values()]
NODES = INNER + LEAVES
DIRS = [(1, 0), (3, 0), (0, 1), (0, 3)]


def sign(tree, node):
    return node if tree == 0 else ((-node[0]) % SIDE, (-node[1]) % SIDE)


def kernel(
    peer, offset, partner, count, fock, occ, amp, integ, energy, s_row, s_col,
    res_out, new_out,
    own, k_in, srow, scol, cols, slots, inner, packed, full_part, inv_den, res_v, new_v,
    lists, lists_in, lists_s, lists_in_s,
    in_sem, out_sem, list_send, list_recv, list_local, row_send, row_recv, y_send, y_recv, c_send, c_recv,
):
    pair, coup = lax.axis_index("pair"), lax.axis_index("coup")
    y, core = pair // 2, pair % 2
    z, x = coup // SIDE, coup % SIDE

    def coup_at(dz, dx):
        return lax.rem(z + dz, SIDE) * SIDE + lax.rem(x + dx, SIDE)

    def pair_at(dy, dc=0):
        return lax.rem(y + dy, SIDE) * 2 + lax.rem(core + dc, 2)

    loads = [
        pltpu.make_async_copy(amp, own, in_sem.at[0]),
        pltpu.make_async_copy(amp, cols.at[pl.ds(pair * BLOCKS, BLOCKS)], in_sem.at[1]),
        pltpu.make_async_copy(integ, k_in, in_sem.at[2]),
        pltpu.make_async_copy(s_col, scol, in_sem.at[3]),
        pltpu.make_async_copy(s_row, srow, in_sem.at[4]),
    ]
    for load in loads:
        load.start()

    barrier = pltpu.get_barrier_semaphore()
    friends = [(pair, coup_at(*d)) for d in DIRS] + [(pair_at(d), coup) for d in (1, 3)] + [(pair_at(0, 1), coup)]
    for friend in friends:
        pl.semaphore_signal(barrier, inc=1, device_id=friend, device_id_type=MESH)
    pl.semaphore_wait(barrier, len(friends))

    def rows_of(tree):
        return pl.ds(tree * HALF, HALF)

    def row_copy(tree, node):
        at, to = sign(tree, TREE[node]), sign(tree, node)
        step = ((to[0] - at[0]) % SIDE, (to[1] - at[1]) % SIDE)
        source = coup_at((-at[0]) % SIDE, (-at[1]) % SIDE)
        i = NODES.index(node)
        if node in INNER:
            src = amp.at[:, rows_of(tree), :] if at == ROOT else inner[tree * len(INNER) + INNER.index(TREE[node])]
            dst = inner[tree * len(INNER) + i]
        else:
            src = packed.at[tree * len(LEAVES) + LEAVES.index(node)]
            dst = slots.at[pl.ds(source * CAP, CAP), rows_of(tree), :]
        return pltpu.make_async_remote_copy(
            src_ref=src, dst_ref=dst, send_sem=row_send.at[tree, i], recv_sem=row_recv.at[tree, i],
            device_id=(pair, coup_at(*step)), device_id_type=MESH,
        )

    def source_at(tree, node):
        n = sign(tree, node)
        return coup_at((-n[0]) % SIDE, (-n[1]) % SIDE)

    def row_arrival(tree, node):
        i = NODES.index(node)
        if node in INNER:
            dst = inner[tree * len(INNER) + i]
        else:
            dst = slots.at[pl.ds(source_at(tree, node) * CAP, CAP), rows_of(tree), :]
        return pltpu.make_async_remote_copy(
            src_ref=dst, dst_ref=dst, send_sem=row_send.at[tree, i], recv_sem=row_recv.at[tree, i],
            device_id=(pair, coup_at(*DIRS[0])), device_id_type=MESH,
        )

    def col_region(source, part):
        return cols.at[pl.ds(source * BLOCKS + part * 4, 4)]

    def y_copy(dy, part, hop):
        source = pair if hop == 0 else pair_at((-dy) % SIDE)
        src = amp.at[pl.ds(part * 4, 4)] if hop == 0 else col_region(source, part)
        i = (0 if dy == 1 else 3) + (part if hop == 0 else 2)
        return pltpu.make_async_remote_copy(
            src_ref=src, dst_ref=col_region(source, part), send_sem=y_send.at[i], recv_sem=y_recv.at[i],
            device_id=(pair_at(dy), coup), device_id_type=MESH,
        )

    def c_copy(dy, part):
        i = dy * 2 + part
        source = pair_at(dy)
        src = amp.at[pl.ds(part * 4, 4)] if dy == 0 else col_region(source, part)
        return pltpu.make_async_remote_copy(
            src_ref=src, dst_ref=col_region(source, part), send_sem=c_send.at[i], recv_sem=c_recv.at[i],
            device_id=(pair_at(0, 1), coup), device_id_type=MESH,
        )

    started = []

    def start(copy):
        copy.start()
        started.append(copy)

    position = 0

    def send_rows(upto):
        nonlocal position
        while position < upto:
            tree, node = ORDER[position]
            parent = TREE[node]
            if parent != ROOT and (tree, parent) not in arrived:
                arrived.add((tree, parent))
                row_arrival(tree, parent).wait_recv()
            if node in LEAVES:
                pack(tree, node)
            start(row_copy(tree, node))
            position += 1

    arrived = set()

    def pack(tree, node):
        at, to = sign(tree, TREE[node]), sign(tree, node)
        step = ((to[0] - at[0]) % SIDE, (to[1] - at[1]) % SIDE)
        source = coup_at((-at[0]) % SIDE, (-at[1]) % SIDE)
        d = DIRS.index(step)
        for t in range(CAP):
            which = lists_in_s[d, 0, source * CAP + t]
            packed[tree * len(LEAVES) + LEAVES.index(node), t] = block_of(tree, TREE[node], which)

    def block_of(tree, node, which):
        if node == ROOT:
            return own[which, rows_of(tree), :]
        return inner[tree * len(INNER) + INNER.index(node)][which]

    def keep(tree, node):
        source = source_at(tree, node)
        for t in range(CAP):
            which = lists_s[0, source * CAP + t]
            slots[source * CAP + t, rows_of(tree), :] = block_of(tree, node, which)

    send_rows(4)
    start(y_copy(1, 0, 0))
    start(y_copy(3, 1, 0))
    start(y_copy(1, 1, 0))
    start(y_copy(3, 0, 0))
    start(c_copy(0, 0))
    start(c_copy(0, 1))

    lane = lax.broadcasted_iota(jnp.int32, (1, 128), 1)

    def peers_step(r, peers):
        return jnp.where(lane == r, peer[r // LINKS, r % LINKS], peers)

    peers = lax.fori_loop(0, TASKS, peers_step, jnp.full((1, 128), -1, jnp.int32))

    def list_step(r, carry):
        wanted, row_of, counts, rank = carry
        p = peer[r // LINKS, r % LINKS]
        local = (r // LINKS // 2) * 2 + offset[r // LINKS, r % LINKS]
        match = (lane // CAP) == p
        hit = match & (lane % CAP == counts)
        return (
            jnp.where(hit, local, wanted),
            jnp.where(hit, r, row_of),
            jnp.where(match, counts + 1, counts),
            rank + jnp.where((lane > r) & (peers == p), 1, 0),
        )

    zero = jnp.zeros((1, 128), jnp.int32)
    wanted, row_of, _, rank = lax.fori_loop(0, TASKS, list_step, (zero, zero, zero, zero))
    lists[0:1, :] = wanted
    lists[1:2, :] = row_of
    lists[2:3, :] = jnp.maximum(peers, 0) * CAP + rank

    def list_copy(i):
        return pltpu.make_async_remote_copy(
            src_ref=lists, dst_ref=lists_in.at[i], send_sem=list_send.at[i], recv_sem=list_recv.at[i],
            device_id=(pair, coup_at((-DIRS[i][0]) % SIDE, (-DIRS[i][1]) % SIDE)), device_id_type=MESH,
        )

    for i in range(4):
        start(list_copy(i))
    to_scalars = pltpu.make_async_copy(lists, lists_s, list_local.at[4])
    to_scalars.start()

    for load in loads[:3]:
        load.wait()

    def first_part(p, _):
        e = energy[pl.ds(p, 1), :]
        across = jnp.broadcast_to(e, (V, V))
        i, j = pair * 4 + p // 2, coup * 2 + p % 2
        den = across + across.T - occ[i] - occ[j]
        cur = own[p].astype(jnp.float32)
        full_part[p] = k_in[p].astype(jnp.float32) + den * cur
        inv_den[p] = 1.0 / den
        return 0

    lax.fori_loop(0, 4, first_part, 0)
    to_scalars.wait()
    moves = []
    for i in range(4):
        list_copy(i).wait_recv()
        moves.append(pltpu.make_async_copy(lists_in.at[i], lists_in_s.at[i], list_local.at[i]))
        moves[-1].start()
    for move in moves:
        move.wait()

    send_rows(8)
    lax.fori_loop(4, 8, first_part, 0)
    for t in range(CAP):
        slots[coup * CAP + t] = own[lists_s[0, coup * CAP + t]]

    def product(a, b, transposed=False):
        dims = (((1,), (1 if transposed else 0,)), ((), ()))
        return lax.dot_general(a, b, dims, preferred_element_type=jnp.float32)

    def row_first(source):
        def body(h, _):
            for u in range(2):
                slot = source * CAP + h * 2 + u
                r = lists_s[1, slot]
                k = source * 2 + lists_s[0, slot] % 2
                f = fock[k, coup * 2 + (r // LINKS) % 2]
                slots[slot] = (f * product(srow[r], slots[slot])).astype(jnp.bfloat16)
            return 0

        lax.fori_loop(0, CAP // 2, body, 0)

    def col_pair(p, _):
        i, parity = pair * 4 + p // 2, p % 2
        parts = []
        for s in range(LINKS):
            q = partner[p, s]
            t = cols[(q // 4) * BLOCKS + (q % 4) * 2 + parity]
            parts.append((fock[i, q] * product(scol[p * LINKS + s], t)).astype(jnp.bfloat16))
        total = jnp.zeros((V, V), jnp.float32)
        for s in range(LINKS):
            total = total + product(parts[s], scol[p * LINKS + s], True)
        full_part[p] = full_part[p] - total
        return 0

    y_copy(1, 0, 0).wait_recv()
    start(y_copy(1, 0, 1))
    start(c_copy(3, 0))
    y_copy(3, 1, 0).wait_recv()
    start(y_copy(3, 1, 1))
    start(c_copy(1, 1))
    loads[3].wait()
    loads[4].wait()
    row_first(coup)
    send_rows(12)
    for n in ((0, 1), (3, 0)):
        for tree in range(2):
            keep(tree, n)
    y_copy(1, 1, 0).wait_recv()
    start(c_copy(3, 1))
    y_copy(3, 0, 0).wait_recv()
    start(c_copy(1, 0))
    send_rows(16)
    for n in ((1, 1), (3, 3)):
        for tree in range(2):
            row_arrival(tree, n).wait_recv()
            arrived.add((tree, n))
            keep(tree, n)
    send_rows(20)
    y_copy(1, 0, 1).wait_recv()
    start(c_copy(2, 0))
    y_copy(3, 1, 1).wait_recv()
    start(c_copy(2, 1))
    leaf_done = set()

    def source_ready(*nodes):
        for n in nodes:
            for tree in range(2):
                m = sign(tree, n)
                if m in LEAVES and (tree, m) not in leaf_done:
                    leaf_done.add((tree, m))
                    row_arrival(tree, m).wait_recv()

    send_rows(22)
    for dy in range(4):
        for part in range(2):
            c_copy(dy, part).wait_recv()
    lax.fori_loop(0, 4, col_pair, 0)
    send_rows(26)
    lax.fori_loop(4, 8, col_pair, 0)
    send_rows(30)
    for tree in range(2):
        keep(tree, (1, 2))
    for n in ((0, 1), (0, 3), (1, 0), (3, 0), (0, 2), (2, 0), (1, 1), (3, 3), (2, 1), (2, 3), (1, 3), (3, 1), (1, 2), (3, 2), (2, 2)):
        source_ready(n)
        row_first(coup_at((-n[0]) % SIDE, (-n[1]) % SIDE))

    def outs(p):
        return [
            pltpu.make_async_copy(res_v.at[p], res_out.at[p], out_sem.at[0, p]),
            pltpu.make_async_copy(new_v.at[p], new_out.at[p], out_sem.at[1, p]),
        ]

    row_id = lax.broadcasted_iota(jnp.int32, (V, 1), 0)
    col_id = lax.broadcasted_iota(jnp.int32, (1, V), 1)

    def last_part(p, _):
        total = jnp.zeros((V, V), jnp.float32)
        for s in range(LINKS):
            r = p * LINKS + s
            total = total + product(slots[lists_s[2, r]], srow[r], True)
        full = full_part[p] - total
        n = count[p]
        mask = (row_id < n).astype(jnp.float32) * (col_id < n).astype(jnp.float32)
        res_v[p] = (mask * full).astype(jnp.bfloat16)
        new_v[p] = (mask * (own[p].astype(jnp.float32) - full * inv_den[p])).astype(jnp.bfloat16)
        for copy in outs(p):
            copy.start()
        return 0

    lax.fori_loop(0, BLOCKS, last_part, 0)
    for copy in started:
        copy.wait_send()
    for p in range(BLOCKS):
        for copy in outs(p):
            copy.wait()


def on_device(
    amplitudes, integrals, pno_energy, occ_energy, occ_fock, row_intersection, column_intersection,
    row_peer, row_offset, column_partner, pno_count,
):
    smem, hbm, vmem = (pl.BlockSpec(memory_space=m) for m in (pltpu.SMEM, pl.ANY, pltpu.VMEM))
    bf16, f32, i32 = jnp.bfloat16, jnp.float32, jnp.int32
    dma = pltpu.SemaphoreType.DMA
    block = (BLOCKS, V, V)
    return pl.pallas_call(
        kernel,
        out_shape=(jax.ShapeDtypeStruct(block, bf16), jax.ShapeDtypeStruct(block, bf16)),
        in_specs=[smem] * 6 + [hbm, hbm, vmem, hbm, hbm],
        out_specs=(hbm, hbm),
        scratch_shapes=[
            pltpu.VMEM(block, bf16),
            pltpu.VMEM(block, bf16),
            pltpu.VMEM((TASKS, V, V), bf16),
            pltpu.VMEM((TASKS, V, V), bf16),
            pltpu.VMEM((8 * BLOCKS, V, V), bf16),
            pltpu.VMEM((N_COUP * CAP, V, V), bf16),
            [pltpu.VMEM((BLOCKS, HALF, V), bf16)] * (2 * len(INNER)),
            pltpu.VMEM((2 * len(LEAVES), CAP, HALF, V), bf16),
            pltpu.VMEM(block, f32),
            pltpu.VMEM(block, f32),
            pltpu.VMEM(block, bf16),
            pltpu.VMEM(block, bf16),
            pltpu.VMEM((8, 128), i32),
            pltpu.VMEM((4, 8, 128), i32),
            pltpu.SMEM((8, 128), i32),
            pltpu.SMEM((4, 8, 128), i32),
            dma((5,)), dma((2, BLOCKS)), dma((4,)), dma((4,)), dma((5,)),
            dma((2, len(NODES))), dma((2, len(NODES))), dma((6,)), dma((6,)), dma((8,)), dma((8,)),
        ],
        compiler_params=pltpu.CompilerParams(
            collective_id=0, has_side_effects=True, vmem_limit_bytes=62 * 2**20
        ),
        cost_estimate=pl.CostEstimate(flops=96 * 4 * V**3, bytes_accessed=16 * 2**20, transcendentals=0),
        name="residual_iteration",
    )(
        row_peer.reshape(BLOCKS, LINKS), row_offset, column_partner, pno_count, occ_fock, occ_energy,
        amplitudes, integrals, pno_energy,
        row_intersection.reshape(TASKS, V, V), column_intersection.reshape(TASKS, V, V),
    )


def solution(mesh):
    whole = P(("pair", "coup"))
    return jax.shard_map(
        on_device,
        mesh=mesh,
        in_specs=(whole, whole, whole, P(), P(), whole, whole, whole, whole, whole, whole),
        out_specs=(whole, whole),
        check_vma=False,
    )
```

time: 217 us -> 82.9 us (0.38)
  waiting for transfers between devices: 133 us -> 0 us
  Pallas kernels: 0 us -> 76.1 us
  matrix products: 26.3 us -> 0 us
  other arithmetic: 21.5 us -> 0 us
  local copies, waits for them, and re-layouts: 20.5 us -> 5.87 us
  between operations: 14.1 us -> 0.64 us
    all_gather x2 -> x0, waiting for transfers between devices: 131 us -> none  [the longest x1 85.8 us: on_device(): lax.all_gather(amplitudes, 'coup', axis=0, tiled=True)]
    pallas_call x0 -> x1, Pallas kernels: none -> 76.1 us  [on_device(): pl.pallas_call(kernel, out_shape=(jax.ShapeDtypeStruct(block, bf16), jax....]
    dot_general x2 -> x0, matrix products: 26.3 us -> none  [sandwich(): jnp.einsum('nfe,nwe->nfw', central_product, shared_orbitals, preferred_el...]
    gather x2 -> x0, local copies, waits for them, and re-layouts: 19.1 us -> none  [pick_blocks(): picked = jnp.take(piece, jnp.clip(wanted, 0, count - 1), axis=0)]
    reduce_sum x4 -> x0, other arithmetic: 15.2 us -> none  [the longest x1 6.58 us: on_device(): jnp.sum(column_fock_matrix[:, :, None, None] * column_terms, axis=1)]
    unnamed x7 -> x3, local copies, waits for them, and re-layouts: 0.77 us -> 5.87 us
    convert_element_type x2 -> x0, other arithmetic: 3.07 us -> none  [the longest x1 2.34 us: on_device(): (mask * (current - full / energy_denominator)).astype(jnp.bfloat16)]
  transfers between devices with their start and end apart: 2 -> 0, of which waited for: 2 -> 0; matrix products, arithmetic and copies ran while one was open for 17% -> 0% of each run, Pallas kernels for 0% -> 0%
where the time goes in v1:
time: 82.9 us; the launch traced here: 82.6 us
  Pallas kernels  76.1 us (92%)
  local copies, waits for them, and re-layouts  5.87 us (7%)
    pallas_call x1, Pallas kernels, on_device(): pl.pallas_call(kernel, out_shape=(jax.ShapeDtypeStruct(block, bf16), jax....  76.1 us
    unnamed x3, local copies, waits for them, and re-layouts  5.87 us

profile of v1, /device:TPU:0, one launch (start us, length us, event | category | flops | bytes accessed | tf_op | source)
XLA Modules:
  0.0 82.6 jit_solution(746966875879130550)
XLA Ops:
  0.6 1.4 %copy.13 = s32[8,6,1]{1,0,2:T(8,128)} copy(s32[8,6,1]{0,2,1:T(1,128)} %param.18) | data formatting | bytes 384 | tf_op args[7]
  2.0 76.1 %residual_iteration.1 = (bf16[8,256,256]{2,1,0:T(8,128)(2,1)}, bf16[8,256,256]{2,1,0:T(8,128)(2,1)}) custom-call(s32[8,6]{1,0:T(8,128)} %bitcast.3, s32[8,6]{1,0:T(8,128)} %offset.1, s32[8,6]{1,0:T(8,128)} %partner.1, s32[8]{0:T(128)} %count.1, f32[32,32]{1,0:T(8,128)} %fock.1, f32[32]{0:T(128)} %occ.1, bf16[8,256,256]{2,1,0:T(8,128)(2,1)} %amp.1, ...), custom_call_target="tpu_custom_call" | custom-call | flops 6442450944 | bytes 16777216 | tf_op jit(solution)/shard_map/residual_iteration/pallas_call | solution.py:370
  78.0 2.3 %copy.16 = bf16[8,256,256]{2,1,0:T(8,128)(2,1)} copy(bf16[8,256,256]{2,1,0:T(8,128)(2,1)} %get-tuple-element.4) | data formatting | bytes 2097152
  80.3 2.3 %copy.17 = bf16[8,256,256]{2,1,0:T(8,128)(2,1)} copy(bf16[8,256,256]{2,1,0:T(8,128)(2,1)} %get-tuple-element.5) | data formatting | bytes 2097152

commit v2 on v1

--- a/solution.py
+++ b/solution.py
@@ -44,11 +44,12 @@
 
 
 def kernel(
-    peer, offset, partner, count, fock, occ, amp, integ, energy, s_row, s_col,
+    peer_h, offset_h, partner_h, count_h, fock_h, occ_h, energy_h, amp, integ, s_row, s_col,
     res_out, new_out,
+    peer, offset, partner, count, fock, occ, energy,
     own, k_in, srow, scol, cols, slots, inner, packed, full_part, inv_den, res_v, new_v,
     lists, lists_in, lists_s, lists_in_s,
-    in_sem, out_sem, list_send, list_recv, list_local, row_send, row_recv, y_send, y_recv, c_send, c_recv,
+    small_sem, in_sem, out_sem, list_send, list_recv, list_local, row_send, row_recv, y_send, y_recv, c_send, c_recv,
 ):
     pair, coup = lax.axis_index("pair"), lax.axis_index("coup")
     y, core = pair // 2, pair % 2
@@ -60,20 +61,20 @@
     def pair_at(dy, dc=0):
         return lax.rem(y + dy, SIDE) * 2 + lax.rem(core + dc, 2)
 
-    loads = [
-        pltpu.make_async_copy(amp, own, in_sem.at[0]),
-        pltpu.make_async_copy(amp, cols.at[pl.ds(pair * BLOCKS, BLOCKS)], in_sem.at[1]),
-        pltpu.make_async_copy(integ, k_in, in_sem.at[2]),
-        pltpu.make_async_copy(s_col, scol, in_sem.at[3]),
-        pltpu.make_async_copy(s_row, srow, in_sem.at[4]),
+    small = [
+        (peer_h, peer), (offset_h, offset), (partner_h, partner), (count_h, count), (fock_h, fock), (occ_h, occ),
+        (energy_h, energy),
     ]
-    for load in loads:
-        load.start()
+    large = [(amp, own), (amp, cols.at[pl.ds(pair * BLOCKS, BLOCKS)]), (integ, k_in), (s_col, scol), (s_row, srow)]
+    small_loads = [pltpu.make_async_copy(a, b, small_sem.at[i]) for i, (a, b) in enumerate(small)]
+    loads = [pltpu.make_async_copy(a, b, in_sem.at[i]) for i, (a, b) in enumerate(large)]
 
     barrier = pltpu.get_barrier_semaphore()
     friends = [(pair, coup_at(*d)) for d in DIRS] + [(pair_at(d), coup) for d in (1, 3)] + [(pair_at(0, 1), coup)]
     for friend in friends:
         pl.semaphore_signal(barrier, inc=1, device_id=friend, device_id_type=MESH)
+    for load in small_loads:
+        load.start()
     pl.semaphore_wait(barrier, len(friends))
 
     def rows_of(tree):
@@ -181,17 +182,21 @@
     start(y_copy(3, 0, 0))
     start(c_copy(0, 0))
     start(c_copy(0, 1))
+    for load in loads:
+        load.start()
+    for load in small_loads:
+        load.wait()
 
     lane = lax.broadcasted_iota(jnp.int32, (1, 128), 1)
 
     def peers_step(r, peers):
-        return jnp.where(lane == r, peer[r // LINKS, r % LINKS], peers)
+        return jnp.where(lane == r, peer[r % LINKS, 0, r // LINKS], peers)
 
     peers = lax.fori_loop(0, TASKS, peers_step, jnp.full((1, 128), -1, jnp.int32))
 
     def list_step(r, carry):
         wanted, row_of, counts, rank = carry
-        p = peer[r // LINKS, r % LINKS]
+        p = peer[r % LINKS, 0, r // LINKS]
         local = (r // LINKS // 2) * 2 + offset[r // LINKS, r % LINKS]
         match = (lane // CAP) == p
         hit = match & (lane % CAP == counts)
@@ -251,17 +256,20 @@
         dims = (((1,), (1 if transposed else 0,)), ((), ()))
         return lax.dot_general(a, b, dims, preferred_element_type=jnp.float32)
 
-    def row_first(source):
-        def body(h, _):
-            for u in range(2):
-                slot = source * CAP + h * 2 + u
+    def row_first(*nodes):
+        for n in nodes:
+            source_ready(n)
+        for n in nodes:
+            source = coup_at((-n[0]) % SIDE, (-n[1]) % SIDE)
+            for t in range(CAP):
+                slot = source * CAP + t
                 r = lists_s[1, slot]
                 k = source * 2 + lists_s[0, slot] % 2
                 f = fock[k, coup * 2 + (r // LINKS) % 2]
                 slots[slot] = (f * product(srow[r], slots[slot])).astype(jnp.bfloat16)
-            return 0
-
-        lax.fori_loop(0, CAP // 2, body, 0)
+
+    def wide(blocks):
+        return jnp.concatenate(blocks, axis=1)
 
     def col_pair(p, _):
         i, parity = pair * 4 + p // 2, p % 2
@@ -270,63 +278,59 @@
             q = partner[p, s]
             t = cols[(q // 4) * BLOCKS + (q % 4) * 2 + parity]
             parts.append((fock[i, q] * product(scol[p * LINKS + s], t)).astype(jnp.bfloat16))
-        total = jnp.zeros((V, V), jnp.float32)
-        for s in range(LINKS):
-            total = total + product(parts[s], scol[p * LINKS + s], True)
-        full_part[p] = full_part[p] - total
+        intersections = [scol[p * LINKS + s] for s in range(LINKS)]
+        full_part[p] = full_part[p] - product(wide(parts), wide(intersections), True)
         return 0
 
+    leaf_done = set()
+
+    def source_ready(n):
+        for tree in range(2):
+            m = sign(tree, n)
+            if m in LEAVES and (tree, m) not in leaf_done:
+                leaf_done.add((tree, m))
+                row_arrival(tree, m).wait_recv()
+
+    send_rows(16)
     y_copy(1, 0, 0).wait_recv()
     start(y_copy(1, 0, 1))
     start(c_copy(3, 0))
     y_copy(3, 1, 0).wait_recv()
     start(y_copy(3, 1, 1))
     start(c_copy(1, 1))
-    loads[3].wait()
-    loads[4].wait()
-    row_first(coup)
-    send_rows(12)
     for n in ((0, 1), (3, 0)):
         for tree in range(2):
             keep(tree, n)
+    loads[4].wait()
+    row_first(ROOT)
+    row_first((0, 1), (0, 3))
+    row_first((1, 0), (3, 0))
     y_copy(1, 1, 0).wait_recv()
     start(c_copy(3, 1))
     y_copy(3, 0, 0).wait_recv()
     start(c_copy(1, 0))
-    send_rows(16)
+    send_rows(26)
     for n in ((1, 1), (3, 3)):
         for tree in range(2):
-            row_arrival(tree, n).wait_recv()
-            arrived.add((tree, n))
             keep(tree, n)
-    send_rows(20)
+    row_first((1, 1), (3, 3))
     y_copy(1, 0, 1).wait_recv()
     start(c_copy(2, 0))
     y_copy(3, 1, 1).wait_recv()
     start(c_copy(2, 1))
-    leaf_done = set()
-
-    def source_ready(*nodes):
-        for n in nodes:
-            for tree in range(2):
-                m = sign(tree, n)
-                if m in LEAVES and (tree, m) not in leaf_done:
-                    leaf_done.add((tree, m))
-                    row_arrival(tree, m).wait_recv()
-
-    send_rows(22)
+    row_first((0, 2), (2, 0))
+    loads[3].wait()
     for dy in range(4):
         for part in range(2):
             c_copy(dy, part).wait_recv()
-    lax.fori_loop(0, 4, col_pair, 0)
-    send_rows(26)
-    lax.fori_loop(4, 8, col_pair, 0)
+    lax.fori_loop(0, 5, col_pair, 0)
     send_rows(30)
     for tree in range(2):
         keep(tree, (1, 2))
-    for n in ((0, 1), (0, 3), (1, 0), (3, 0), (0, 2), (2, 0), (1, 1), (3, 3), (2, 1), (2, 3), (1, 3), (3, 1), (1, 2), (3, 2), (2, 2)):
-        source_ready(n)
-        row_first(coup_at((-n[0]) % SIDE, (-n[1]) % SIDE))
+    lax.fori_loop(5, 8, col_pair, 0)
+    row_first((2, 3))
+    row_first((2, 1), (1, 2), (3, 2))
+    row_first((3, 1), (1, 3), (2, 2))
 
     def outs(p):
         return [
@@ -338,11 +342,8 @@
     col_id = lax.broadcasted_iota(jnp.int32, (1, V), 1)
 
     def last_part(p, _):
-        total = jnp.zeros((V, V), jnp.float32)
-        for s in range(LINKS):
-            r = p * LINKS + s
-            total = total + product(slots[lists_s[2, r]], srow[r], True)
-        full = full_part[p] - total
+        rows = [p * LINKS + s for s in range(LINKS)]
+        full = full_part[p] - product(wide([slots[lists_s[2, r]] for r in rows]), wide([srow[r] for r in rows]), True)
         n = count[p]
         mask = (row_id < n).astype(jnp.float32) * (col_id < n).astype(jnp.float32)
         res_v[p] = (mask * full).astype(jnp.bfloat16)
@@ -359,20 +360,39 @@
             copy.wait()
 
 
+def copy_kernel(a, b, a_out, b_out, a_v, b_v, in_sem, out_sem):
+    ways = [(a, a_v, a_out), (b, b_v, b_out)]
+    steps = []
+    for h in range(2):
+        for w, (src, mid, dst) in enumerate(ways):
+            part = pl.ds(h * BLOCKS // 2, BLOCKS // 2)
+            load = pltpu.make_async_copy(src.at[part], mid.at[part], in_sem.at[w, h])
+            store = pltpu.make_async_copy(mid.at[part], dst.at[part], out_sem.at[w, h])
+            load.start()
+            steps.append((load, store))
+    for load, store in steps:
+        load.wait()
+        store.start()
+    for _, store in steps:
+        store.wait()
+
+
 def on_device(
     amplitudes, integrals, pno_energy, occ_energy, occ_fock, row_intersection, column_intersection,
     row_peer, row_offset, column_partner, pno_count,
 ):
-    smem, hbm, vmem = (pl.BlockSpec(memory_space=m) for m in (pltpu.SMEM, pl.ANY, pltpu.VMEM))
+    hbm = pl.BlockSpec(memory_space=pl.ANY)
     bf16, f32, i32 = jnp.bfloat16, jnp.float32, jnp.int32
     dma = pltpu.SemaphoreType.DMA
     block = (BLOCKS, V, V)
-    return pl.pallas_call(
+    residual, new = pl.pallas_call(
         kernel,
         out_shape=(jax.ShapeDtypeStruct(block, bf16), jax.ShapeDtypeStruct(block, bf16)),
-        in_specs=[smem] * 6 + [hbm, hbm, vmem, hbm, hbm],
+        in_specs=[hbm] * 11,
         out_specs=(hbm, hbm),
         scratch_shapes=[
+            pltpu.SMEM((LINKS, 1, BLOCKS), i32), pltpu.SMEM((BLOCKS, LINKS), i32), pltpu.SMEM((BLOCKS, LINKS), i32),
+            pltpu.SMEM((BLOCKS,), i32), pltpu.SMEM((32, 32), f32), pltpu.SMEM((32,), f32), pltpu.VMEM((BLOCKS, V), f32),
             pltpu.VMEM(block, bf16),
             pltpu.VMEM(block, bf16),
             pltpu.VMEM((TASKS, V, V), bf16),
@@ -389,7 +409,7 @@
             pltpu.VMEM((4, 8, 128), i32),
             pltpu.SMEM((8, 128), i32),
             pltpu.SMEM((4, 8, 128), i32),
-            dma((5,)), dma((2, BLOCKS)), dma((4,)), dma((4,)), dma((5,)),
+            dma((7,)), dma((5,)), dma((2, BLOCKS)), dma((4,)), dma((4,)), dma((5,)),
             dma((2, len(NODES))), dma((2, len(NODES))), dma((6,)), dma((6,)), dma((8,)), dma((8,)),
         ],
         compiler_params=pltpu.CompilerParams(
@@ -398,10 +418,20 @@
         cost_estimate=pl.CostEstimate(flops=96 * 4 * V**3, bytes_accessed=16 * 2**20, transcendentals=0),
         name="residual_iteration",
     )(
-        row_peer.reshape(BLOCKS, LINKS), row_offset, column_partner, pno_count, occ_fock, occ_energy,
-        amplitudes, integrals, pno_energy,
+        jnp.transpose(row_peer, (1, 2, 0)), row_offset, column_partner, pno_count, occ_fock, occ_energy, pno_energy,
+        amplitudes, integrals,
         row_intersection.reshape(TASKS, V, V), column_intersection.reshape(TASKS, V, V),
     )
+    return pl.pallas_call(
+        copy_kernel,
+        out_shape=(jax.ShapeDtypeStruct(block, bf16), jax.ShapeDtypeStruct(block, bf16)),
+        in_specs=[hbm, hbm],
+        out_specs=(hbm, hbm),
+        scratch_shapes=[pltpu.VMEM(block, bf16), pltpu.VMEM(block, bf16), dma((2, 2)), dma((2, 2))],
+        compiler_params=pltpu.CompilerParams(vmem_limit_bytes=62 * 2**20),
+        cost_estimate=pl.CostEstimate(flops=0, bytes_accessed=4 * 2**20, transcendentals=0),
+        name="results",
+    )(residual, new)
 
 
 def solution(mesh):

time: 82.9 us -> 76.9 us (0.928)
  local copies, waits for them, and re-layouts: 5.87 us -> 0 us
    unnamed x3 -> x0, local copies, waits for them, and re-layouts: 5.87 us -> none
    pallas_call x0 -> x1, Pallas kernels: none -> 2.42 us  [on_device(): pl.pallas_call(copy_kernel, out_shape=(jax.ShapeDtypeStruct(block, bf16),...]
    pallas_call x1, Pallas kernels: 76.1 us -> 73.7 us  [on_device(): pl.pallas_call(kernel, out_shape=(jax.ShapeDtypeStruct(block, bf16), jax....]
where the time goes in v2:
time: 76.9 us; the launch traced here: 76.8 us
  Pallas kernels  76.1 us (99%)
    pallas_call x1, Pallas kernels, on_device(): pl.pallas_call(kernel, out_shape=(jax.ShapeDtypeStruct(block, bf16), jax....  73.7 us
    pallas_call x1, Pallas kernels, on_device(): pl.pallas_call(copy_kernel, out_shape=(jax.ShapeDtypeStruct(block, bf16),...  2.42 us

profile of v2, /device:TPU:0, one launch (start us, length us, event | category | flops | bytes accessed | tf_op | source)
XLA Modules:
  0.0 76.8 jit_solution(17574259301734105281)
XLA Ops:
  0.6 73.7 %residual_iteration.1 = (bf16[8,256,256]{2,1,0:T(8,128)(2,1)}, bf16[8,256,256]{2,1,0:T(8,128)(2,1)}) custom-call(s32[6,1,8]{2,1,0:T(1,128)} %bitcast.5, s32[8,6]{1,0:T(8,128)} %offset_h.1, s32[8,6]{1,0:T(8,128)} %partner_h.1, s32[8]{0:T(128)} %count_h.1, f32[32,32]{1,0:T(8,128)} %fock_h.1, f32[32]{0:T(128)} %occ_h.1, f32[8,256]{1,0:T(8,128)} %energy_h.1, ...), custom_call_target="tpu_custom_call" | custom-call | flops 6442450944 | bytes 16777216 | tf_op jit(solution)/shard_map/residual_iteration/pallas_call | solution.py:388
  74.3 2.4 %results.1 = (bf16[8,256,256]{2,1,0:T(8,128)(2,1)}, bf16[8,256,256]{2,1,0:T(8,128)(2,1)}) custom-call(bf16[8,256,256]{2,1,0:T(8,128)(2,1)} %get-tuple-element.4.a, bf16[8,256,256]{2,1,0:T(8,128)(2,1)} %get-tuple-element.5.b), custom_call_target="tpu_custom_call" | custom-call | bytes 4194304 | tf_op jit(solution)/shard_map/results/pallas_call | solution.py:425

commit v3 on v2

--- a/solution.py
+++ b/solution.py
@@ -45,11 +45,11 @@
 
 def kernel(
     peer_h, offset_h, partner_h, count_h, fock_h, occ_h, energy_h, amp, integ, s_row, s_col,
-    res_out, new_out,
+    res_v, new_v,
     peer, offset, partner, count, fock, occ, energy,
-    own, k_in, srow, scol, cols, slots, inner, packed, full_part, inv_den, res_v, new_v,
+    own, k_in, srow, scol, cols, slots, inner, packed, full_part, inv_den,
     lists, lists_in, lists_s, lists_in_s,
-    small_sem, in_sem, out_sem, list_send, list_recv, list_local, row_send, row_recv, y_send, y_recv, c_send, c_recv,
+    small_sem, in_sem, list_send, list_recv, list_local, row_send, row_recv, y_send, y_recv, c_send, c_recv,
 ):
     pair, coup = lax.axis_index("pair"), lax.axis_index("coup")
     y, core = pair // 2, pair % 2
@@ -332,48 +332,28 @@
     row_first((2, 1), (1, 2), (3, 2))
     row_first((3, 1), (1, 3), (2, 2))
 
-    def outs(p):
-        return [
-            pltpu.make_async_copy(res_v.at[p], res_out.at[p], out_sem.at[0, p]),
-            pltpu.make_async_copy(new_v.at[p], new_out.at[p], out_sem.at[1, p]),
-        ]
-
     row_id = lax.broadcasted_iota(jnp.int32, (V, 1), 0)
     col_id = lax.broadcasted_iota(jnp.int32, (1, V), 1)
 
-    def last_part(p, _):
+    def last_part(p):
         rows = [p * LINKS + s for s in range(LINKS)]
         full = full_part[p] - product(wide([slots[lists_s[2, r]] for r in rows]), wide([srow[r] for r in rows]), True)
         n = count[p]
         mask = (row_id < n).astype(jnp.float32) * (col_id < n).astype(jnp.float32)
         res_v[p] = (mask * full).astype(jnp.bfloat16)
         new_v[p] = (mask * (own[p].astype(jnp.float32) - full * inv_den[p])).astype(jnp.bfloat16)
-        for copy in outs(p):
-            copy.start()
-        return 0
-
-    lax.fori_loop(0, BLOCKS, last_part, 0)
+
+    for p in range(BLOCKS):
+        last_part(p)
     for copy in started:
         copy.wait_send()
-    for p in range(BLOCKS):
-        for copy in outs(p):
-            copy.wait()
-
-
-def copy_kernel(a, b, a_out, b_out, a_v, b_v, in_sem, out_sem):
-    ways = [(a, a_v, a_out), (b, b_v, b_out)]
-    steps = []
-    for h in range(2):
-        for w, (src, mid, dst) in enumerate(ways):
-            part = pl.ds(h * BLOCKS // 2, BLOCKS // 2)
-            load = pltpu.make_async_copy(src.at[part], mid.at[part], in_sem.at[w, h])
-            store = pltpu.make_async_copy(mid.at[part], dst.at[part], out_sem.at[w, h])
-            load.start()
-            steps.append((load, store))
-    for load, store in steps:
-        load.wait()
+
+
+def copy_kernel(a, b, a_out, b_out, sem):
+    stores = [pltpu.make_async_copy(a, a_out, sem.at[0]), pltpu.make_async_copy(b, b_out, sem.at[1])]
+    for store in stores:
         store.start()
-    for _, store in steps:
+    for store in stores:
         store.wait()
 
 
@@ -381,15 +361,15 @@
     amplitudes, integrals, pno_energy, occ_energy, occ_fock, row_intersection, column_intersection,
     row_peer, row_offset, column_partner, pno_count,
 ):
-    hbm = pl.BlockSpec(memory_space=pl.ANY)
+    hbm, vmem = pl.BlockSpec(memory_space=pl.ANY), pl.BlockSpec(memory_space=pltpu.VMEM)
     bf16, f32, i32 = jnp.bfloat16, jnp.float32, jnp.int32
     dma = pltpu.SemaphoreType.DMA
     block = (BLOCKS, V, V)
     residual, new = pl.pallas_call(
         kernel,
-        out_shape=(jax.ShapeDtypeStruct(block, bf16), jax.ShapeDtypeStruct(block, bf16)),
+        out_shape=(pltpu.VMEM(block, bf16), pltpu.VMEM(block, bf16)),
         in_specs=[hbm] * 11,
-        out_specs=(hbm, hbm),
+        out_specs=(vmem, vmem),
         scratch_shapes=[
             pltpu.SMEM((LINKS, 1, BLOCKS), i32), pltpu.SMEM((BLOCKS, LINKS), i32), pltpu.SMEM((BLOCKS, LINKS), i32),
             pltpu.SMEM((BLOCKS,), i32), pltpu.SMEM((32, 32), f32), pltpu.SMEM((32,), f32), pltpu.VMEM((BLOCKS, V), f32),
@@ -403,17 +383,15 @@
             pltpu.VMEM((2 * len(LEAVES), CAP, HALF, V), bf16),
             pltpu.VMEM(block, f32),
             pltpu.VMEM(block, f32),
-            pltpu.VMEM(block, bf16),
-            pltpu.VMEM(block, bf16),
             pltpu.VMEM((8, 128), i32),
             pltpu.VMEM((4, 8, 128), i32),
             pltpu.SMEM((8, 128), i32),
             pltpu.SMEM((4, 8, 128), i32),
-            dma((7,)), dma((5,)), dma((2, BLOCKS)), dma((4,)), dma((4,)), dma((5,)),
+            dma((7,)), dma((5,)), dma((4,)), dma((4,)), dma((5,)),
             dma((2, len(NODES))), dma((2, len(NODES))), dma((6,)), dma((6,)), dma((8,)), dma((8,)),
         ],
         compiler_params=pltpu.CompilerParams(
-            collective_id=0, has_side_effects=True, vmem_limit_bytes=62 * 2**20
+            collective_id=0, has_side_effects=True, vmem_limit_bytes=54 * 2**20
         ),
         cost_estimate=pl.CostEstimate(flops=96 * 4 * V**3, bytes_accessed=16 * 2**20, transcendentals=0),
         name="residual_iteration",
@@ -425,13 +403,13 @@
     return pl.pallas_call(
         copy_kernel,
         out_shape=(jax.ShapeDtypeStruct(block, bf16), jax.ShapeDtypeStruct(block, bf16)),
-        in_specs=[hbm, hbm],
+        in_specs=[vmem, vmem],
         out_specs=(hbm, hbm),
-        scratch_shapes=[pltpu.VMEM(block, bf16), pltpu.VMEM(block, bf16), dma((2, 2)), dma((2, 2))],
-        compiler_params=pltpu.CompilerParams(vmem_limit_bytes=62 * 2**20),
+        scratch_shapes=[dma((2,))],
+        compiler_params=pltpu.CompilerParams(vmem_limit_bytes=54 * 2**20),
         cost_estimate=pl.CostEstimate(flops=0, bytes_accessed=4 * 2**20, transcendentals=0),
         name="results",
-    )(residual, new)
+    )(*(pltpu.with_memory_space_constraint(a, pltpu.VMEM) for a in (residual, new)))
 
 
 def solution(mesh):

time: 76.9 us -> 73.8 us (0.960)
  Pallas kernels: 76.1 us -> 73 us
    pallas_call x1, Pallas kernels: 73.7 us -> 71.7 us  [on_device(): pl.pallas_call(kernel, out_shape=(pltpu.VMEM(block, bf16), pltpu.VMEM(blo...]
    pallas_call x1, Pallas kernels: 2.42 us -> 1.33 us  [on_device(): pl.pallas_call(copy_kernel, out_shape=(jax.ShapeDtypeStruct(block, bf16),...]
where the time goes in v3:
time: 73.8 us; the launch traced here: 73.7 us
  Pallas kernels  73 us (99%)
    pallas_call x1, Pallas kernels, on_device(): pl.pallas_call(kernel, out_shape=(pltpu.VMEM(block, bf16), pltpu.VMEM(blo...  71.7 us

profile of v3, /device:TPU:0, one launch (start us, length us, event | category | flops | bytes accessed | tf_op | source)
XLA Modules:
  0.0 73.7 jit_solution(11673626615900606790)
XLA Ops:
  0.6 71.7 %residual_iteration.1 = (bf16[8,256,256]{2,1,0:T(8,128)(2,1)S(1)}, bf16[8,256,256]{2,1,0:T(8,128)(2,1)S(1)}) custom-call(s32[6,1,8]{2,1,0:T(1,128)} %bitcast.5, s32[8,6]{1,0:T(8,128)} %offset_h.1, s32[8,6]{1,0:T(8,128)} %partner_h.1, s32[8]{0:T(128)} %count_h.1, f32[32,32]{1,0:T(8,128)} %fock_h.1, f32[32]{0:T(128)} %occ_h.1, f32[8,256]{1,0:T(8,128)} %energy_h.1, ...), custom_call_target="tpu_custom_call" | custom-call | flops 6442450944 | bytes 16777216 | tf_op jit(solution)/shard_map/residual_iteration/pallas_call | solution.py:368
  72.3 1.3 %results.1 = (bf16[8,256,256]{2,1,0:T(8,128)(2,1)}, bf16[8,256,256]{2,1,0:T(8,128)(2,1)}) custom-call(bf16[8,256,256]{2,1,0:T(8,128)(2,1)S(1)} %get-tuple-element.4.a, bf16[8,256,256]{2,1,0:T(8,128)(2,1)S(1)} %get-tuple-element.5.b), custom_call_target="tpu_custom_call" | custom-call | bytes 4194304 | tf_op jit(solution)/shard_map/results/pallas_call | solution.py:403

commit v4 on v3

--- a/solution.py
+++ b/solution.py
@@ -24,14 +24,16 @@
 }
 ROOT = (0, 0)
 ORDER = [
-    (0, (0, 1)), (1, (0, 1)), (0, (3, 0)), (1, (3, 0)),
-    (0, (0, 3)), (0, (1, 0)), (1, (0, 3)), (1, (1, 0)),
-    (0, (1, 1)), (1, (1, 1)), (0, (3, 3)), (1, (3, 3)),
-    (0, (0, 2)), (0, (2, 0)), (1, (0, 2)), (1, (2, 0)),
-    (0, (1, 2)), (1, (1, 2)), (0, (2, 1)), (0, (2, 3)),
-    (0, (3, 1)), (1, (2, 1)),
-    (0, (3, 2)), (1, (2, 3)), (1, (3, 1)), (1, (3, 2)),
-    (0, (1, 3)), (0, (2, 2)), (1, (1, 3)), (1, (2, 2)),
+    (0, (0, 1), 0), (1, (0, 1), 0), (0, (3, 0), 0), (1, (3, 0), 0),
+    (0, (0, 1), 1), (1, (0, 1), 1), (0, (3, 0), 1), (1, (3, 0), 1),
+    (0, (1, 1), 0), (1, (1, 1), 0), (0, (3, 3), 0), (1, (3, 3), 0),
+    (0, (1, 1), 1), (1, (1, 1), 1), (0, (3, 3), 1), (1, (3, 3), 1),
+    (0, (1, 2), 0), (1, (1, 2), 0), (0, (1, 0), None), (1, (1, 0), None),
+    (0, (1, 2), 1), (1, (1, 2), 1), (0, (2, 0), None), (1, (2, 0), None),
+    (0, (2, 1), None), (1, (2, 1), None), (0, (0, 3), None), (1, (0, 3), None),
+    (0, (2, 3), None), (1, (2, 3), None), (0, (3, 2), None), (1, (3, 2), None),
+    (0, (3, 1), None), (1, (3, 1), None), (0, (1, 3), None), (1, (1, 3), None),
+    (0, (0, 2), None), (1, (0, 2), None), (0, (2, 2), None), (1, (2, 2), None),
 ]
 INNER = [n for n in TREE if n in TREE.values()]
 LEAVES = [n for n in TREE if n not in TREE.values()]
@@ -80,19 +82,20 @@
     def rows_of(tree):
         return pl.ds(tree * HALF, HALF)
 
-    def row_copy(tree, node):
+    def row_copy(tree, node, part):
         at, to = sign(tree, TREE[node]), sign(tree, node)
         step = ((to[0] - at[0]) % SIDE, (to[1] - at[1]) % SIDE)
         source = coup_at((-at[0]) % SIDE, (-at[1]) % SIDE)
-        i = NODES.index(node)
         if node in INNER:
-            src = amp.at[:, rows_of(tree), :] if at == ROOT else inner[tree * len(INNER) + INNER.index(TREE[node])]
-            dst = inner[tree * len(INNER) + i]
+            four = pl.ds(part * 4, 4)
+            src = amp.at[four, rows_of(tree), :] if at == ROOT else inner_of(tree, TREE[node]).at[four]
+            dst = inner_of(tree, node).at[four]
         else:
             src = packed.at[tree * len(LEAVES) + LEAVES.index(node)]
             dst = slots.at[pl.ds(source * CAP, CAP), rows_of(tree), :]
+        i = NODES.index(node)
         return pltpu.make_async_remote_copy(
-            src_ref=src, dst_ref=dst, send_sem=row_send.at[tree, i], recv_sem=row_recv.at[tree, i],
+            src_ref=src, dst_ref=dst, send_sem=row_send.at[tree, i, part or 0], recv_sem=row_recv.at[tree, i, part or 0],
             device_id=(pair, coup_at(*step)), device_id_type=MESH,
         )
 
@@ -100,14 +103,17 @@
         n = sign(tree, node)
         return coup_at((-n[0]) % SIDE, (-n[1]) % SIDE)
 
-    def row_arrival(tree, node):
+    def inner_of(tree, node):
+        return inner[tree * len(INNER) + INNER.index(node)]
+
+    def row_arrival(tree, node, part):
         i = NODES.index(node)
         if node in INNER:
-            dst = inner[tree * len(INNER) + i]
+            dst = inner_of(tree, node).at[pl.ds(part * 4, 4)]
         else:
             dst = slots.at[pl.ds(source_at(tree, node) * CAP, CAP), rows_of(tree), :]
         return pltpu.make_async_remote_copy(
-            src_ref=dst, dst_ref=dst, send_sem=row_send.at[tree, i], recv_sem=row_recv.at[tree, i],
+            src_ref=dst, dst_ref=dst, send_sem=row_send.at[tree, i, part or 0], recv_sem=row_recv.at[tree, i, part or 0],
             device_id=(pair, coup_at(*DIRS[0])), device_id_type=MESH,
         )
 
@@ -139,21 +145,24 @@
         started.append(copy)
 
     position = 0
+    arrived = set()
+
+    def await_rows(tree, node, part):
+        if (tree, node, part) not in arrived:
+            arrived.add((tree, node, part))
+            row_arrival(tree, node, part).wait_recv()
 
     def send_rows(upto):
         nonlocal position
         while position < upto:
-            tree, node = ORDER[position]
-            parent = TREE[node]
-            if parent != ROOT and (tree, parent) not in arrived:
-                arrived.add((tree, parent))
-                row_arrival(tree, parent).wait_recv()
+            tree, node, part = ORDER[position]
+            if TREE[node] != ROOT:
+                for half in (0, 1) if part is None else (part,):
+                    await_rows(tree, TREE[node], half)
             if node in LEAVES:
                 pack(tree, node)
-            start(row_copy(tree, node))
+            start(row_copy(tree, node, part))
             position += 1
-
-    arrived = set()
 
     def pack(tree, node):
         at, to = sign(tree, TREE[node]), sign(tree, node)
@@ -167,15 +176,17 @@
     def block_of(tree, node, which):
         if node == ROOT:
             return own[which, rows_of(tree), :]
-        return inner[tree * len(INNER) + INNER.index(node)][which]
+        return inner_of(tree, node)[which]
 
     def keep(tree, node):
         source = source_at(tree, node)
+        for half in range(2):
+            await_rows(tree, node, half)
         for t in range(CAP):
             which = lists_s[0, source * CAP + t]
             slots[source * CAP + t, rows_of(tree), :] = block_of(tree, node, which)
 
-    send_rows(4)
+    send_rows(8)
     start(y_copy(1, 0, 0))
     start(y_copy(3, 1, 0))
     start(y_copy(1, 1, 0))
@@ -192,7 +203,7 @@
     def peers_step(r, peers):
         return jnp.where(lane == r, peer[r % LINKS, 0, r // LINKS], peers)
 
-    peers = lax.fori_loop(0, TASKS, peers_step, jnp.full((1, 128), -1, jnp.int32))
+    peers = lax.fori_loop(0, TASKS, peers_step, jnp.full((1, 128), -1, jnp.int32), unroll=8)
 
     def list_step(r, carry):
         wanted, row_of, counts, rank = carry
@@ -208,7 +219,7 @@
         )
 
     zero = jnp.zeros((1, 128), jnp.int32)
-    wanted, row_of, _, rank = lax.fori_loop(0, TASKS, list_step, (zero, zero, zero, zero))
+    wanted, row_of, _, rank = lax.fori_loop(0, TASKS, list_step, (zero, zero, zero, zero), unroll=8)
     lists[0:1, :] = wanted
     lists[1:2, :] = row_of
     lists[2:3, :] = jnp.maximum(peers, 0) * CAP + rank
@@ -223,6 +234,8 @@
         start(list_copy(i))
     to_scalars = pltpu.make_async_copy(lists, lists_s, list_local.at[4])
     to_scalars.start()
+
+    send_rows(12)
 
     for load in loads[:3]:
         load.wait()
@@ -237,7 +250,14 @@
         inv_den[p] = 1.0 / den
         return 0
 
-    lax.fori_loop(0, 4, first_part, 0)
+    lax.fori_loop(0, 2, first_part, 0)
+    send_rows(16)
+    y_copy(1, 0, 0).wait_recv()
+    start(y_copy(1, 0, 1))
+    start(c_copy(3, 0))
+    y_copy(3, 1, 0).wait_recv()
+    start(y_copy(3, 1, 1))
+    start(c_copy(1, 1))
     to_scalars.wait()
     moves = []
     for i in range(4):
@@ -247,8 +267,7 @@
     for move in moves:
         move.wait()
 
-    send_rows(8)
-    lax.fori_loop(4, 8, first_part, 0)
+    lax.fori_loop(2, 8, first_part, 0)
     for t in range(CAP):
         slots[coup * CAP + t] = own[lists_s[0, coup * CAP + t]]
 
@@ -289,48 +308,42 @@
             m = sign(tree, n)
             if m in LEAVES and (tree, m) not in leaf_done:
                 leaf_done.add((tree, m))
-                row_arrival(tree, m).wait_recv()
-
-    send_rows(16)
-    y_copy(1, 0, 0).wait_recv()
-    start(y_copy(1, 0, 1))
-    start(c_copy(3, 0))
-    y_copy(3, 1, 0).wait_recv()
-    start(y_copy(3, 1, 1))
-    start(c_copy(1, 1))
+                row_arrival(tree, m, None).wait_recv()
+
     for n in ((0, 1), (3, 0)):
         for tree in range(2):
             keep(tree, n)
+    send_rows(20)
     loads[4].wait()
     row_first(ROOT)
-    row_first((0, 1), (0, 3))
-    row_first((1, 0), (3, 0))
     y_copy(1, 1, 0).wait_recv()
     start(c_copy(3, 1))
     y_copy(3, 0, 0).wait_recv()
     start(c_copy(1, 0))
-    send_rows(26)
+    send_rows(34)
     for n in ((1, 1), (3, 3)):
         for tree in range(2):
             keep(tree, n)
     row_first((1, 1), (3, 3))
+    row_first((1, 0), (3, 0))
+    loads[3].wait()
+    send_rows(40)
     y_copy(1, 0, 1).wait_recv()
     start(c_copy(2, 0))
     y_copy(3, 1, 1).wait_recv()
     start(c_copy(2, 1))
-    row_first((0, 2), (2, 0))
-    loads[3].wait()
+    for tree in range(2):
+        keep(tree, (1, 2))
+    row_first((2, 0))
     for dy in range(4):
         for part in range(2):
             c_copy(dy, part).wait_recv()
-    lax.fori_loop(0, 5, col_pair, 0)
-    send_rows(30)
-    for tree in range(2):
-        keep(tree, (1, 2))
-    lax.fori_loop(5, 8, col_pair, 0)
-    row_first((2, 3))
-    row_first((2, 1), (1, 2), (3, 2))
-    row_first((3, 1), (1, 3), (2, 2))
+    lax.fori_loop(0, 3, col_pair, 0)
+    row_first((0, 1), (0, 3))
+    lax.fori_loop(3, 8, col_pair, 0)
+    row_first((2, 1), (2, 3), (1, 2), (3, 2))
+    row_first((1, 3), (3, 1))
+    row_first((0, 2), (2, 2))
 
     row_id = lax.broadcasted_iota(jnp.int32, (V, 1), 0)
     col_id = lax.broadcasted_iota(jnp.int32, (1, V), 1)
@@ -388,7 +401,7 @@
             pltpu.SMEM((8, 128), i32),
             pltpu.SMEM((4, 8, 128), i32),
             dma((7,)), dma((5,)), dma((4,)), dma((4,)), dma((5,)),
-            dma((2, len(NODES))), dma((2, len(NODES))), dma((6,)), dma((6,)), dma((8,)), dma((8,)),
+            dma((2, len(NODES), 2)), dma((2, len(NODES), 2)), dma((6,)), dma((6,)), dma((8,)), dma((8,)),
         ],
         compiler_params=pltpu.CompilerParams(
             collective_id=0, has_side_effects=True, vmem_limit_bytes=54 * 2**20

time: 73.8 us -> 70.7 us (0.958)
  Pallas kernels: 73 us -> 69.9 us
    pallas_call x1, Pallas kernels: 71.7 us -> 68.6 us  [on_device(): pl.pallas_call(kernel, out_shape=(pltpu.VMEM(block, bf16), pltpu.VMEM(blo...]
where the time goes in v4:
time: 70.7 us; the launch traced here: 70.5 us
  Pallas kernels  69.9 us (99%)
    pallas_call x1, Pallas kernels, on_device(): pl.pallas_call(kernel, out_shape=(pltpu.VMEM(block, bf16), pltpu.VMEM(blo...  68.6 us

profile of v4, /device:TPU:0, one launch (start us, length us, event | category | flops | bytes accessed | tf_op | source)
XLA Modules:
  0.0 70.5 jit_solution(1554941809924189869)
XLA Ops:
  0.6 68.6 %residual_iteration.1 = (bf16[8,256,256]{2,1,0:T(8,128)(2,1)S(1)}, bf16[8,256,256]{2,1,0:T(8,128)(2,1)S(1)}) custom-call(s32[6,1,8]{2,1,0:T(1,128)} %bitcast.5, s32[8,6]{1,0:T(8,128)} %offset_h.1, s32[8,6]{1,0:T(8,128)} %partner_h.1, s32[8]{0:T(128)} %count_h.1, f32[32,32]{1,0:T(8,128)} %fock_h.1, f32[32]{0:T(128)} %occ_h.1, f32[8,256]{1,0:T(8,128)} %energy_h.1, ...), custom_call_target="tpu_custom_call" | custom-call | flops 6442450944 | bytes 16777216 | tf_op jit(solution)/shard_map/residual_iteration/pallas_call | solution.py:381
  69.2 1.3 %results.1 = (bf16[8,256,256]{2,1,0:T(8,128)(2,1)}, bf16[8,256,256]{2,1,0:T(8,128)(2,1)}) custom-call(bf16[8,256,256]{2,1,0:T(8,128)(2,1)S(1)} %get-tuple-element.4.a, bf16[8,256,256]{2,1,0:T(8,128)(2,1)S(1)} %get-tuple-element.5.b), custom_call_target="tpu_custom_call" | custom-call | bytes 4194304 | tf_op jit(solution)/shard_map/results/pallas_call | solution.py:416

commit v5 on v4

--- a/solution.py
+++ b/solution.py
@@ -33,8 +33,10 @@
     (0, (2, 1), None), (1, (2, 1), None), (0, (0, 3), None), (1, (0, 3), None),
     (0, (2, 3), None), (1, (2, 3), None), (0, (3, 2), None), (1, (3, 2), None),
     (0, (3, 1), None), (1, (3, 1), None), (0, (1, 3), None), (1, (1, 3), None),
-    (0, (0, 2), None), (1, (0, 2), None), (0, (2, 2), None), (1, (2, 2), None),
+    (0, (0, 2), 0), (1, (0, 2), 0), (0, (2, 2), 0), (1, (2, 2), 0),
+    (0, (0, 2), 1), (1, (0, 2), 1), (0, (2, 2), 1), (1, (2, 2), 1),
 ]
+LAST = [(0, 2), (2, 2)]
 INNER = [n for n in TREE if n in TREE.values()]
 LEAVES = [n for n in TREE if n not in TREE.values()]
 NODES = INNER + LEAVES
@@ -47,9 +49,9 @@
 
 def kernel(
     peer_h, offset_h, partner_h, count_h, fock_h, occ_h, energy_h, amp, integ, s_row, s_col,
-    res_v, new_v,
+    own, full_part, inv_den, late_part, late_pair,
     peer, offset, partner, count, fock, occ, energy,
-    own, k_in, srow, scol, cols, slots, inner, packed, full_part, inv_den,
+    k_in, srow, scol, cols, slots, late, inner, packed,
     lists, lists_in, lists_s, lists_in_s,
     small_sem, in_sem, list_send, list_recv, list_local, row_send, row_recv, y_send, y_recv, c_send, c_recv,
 ):
@@ -81,6 +83,13 @@
 
     def rows_of(tree):
         return pl.ds(tree * HALF, HALF)
+
+    def leaf_place(source, tree, node, part):
+        if part is None:
+            return slots.at[pl.ds(source * CAP, CAP), rows_of(tree), :]
+        if part == 0:
+            return slots.at[pl.ds(source * CAP, 2), rows_of(tree), :]
+        return late.at[pl.ds(LAST.index(node) * 2, 2), rows_of(tree), :]
 
     def row_copy(tree, node, part):
         at, to = sign(tree, TREE[node]), sign(tree, node)
@@ -92,7 +101,9 @@
             dst = inner_of(tree, node).at[four]
         else:
             src = packed.at[tree * len(LEAVES) + LEAVES.index(node)]
-            dst = slots.at[pl.ds(source * CAP, CAP), rows_of(tree), :]
+            if part is not None:
+                src = src.at[pl.ds(part * 2, 2)]
+            dst = leaf_place(source, tree, node, part)
         i = NODES.index(node)
         return pltpu.make_async_remote_copy(
             src_ref=src, dst_ref=dst, send_sem=row_send.at[tree, i, part or 0], recv_sem=row_recv.at[tree, i, part or 0],
@@ -111,7 +122,7 @@
         if node in INNER:
             dst = inner_of(tree, node).at[pl.ds(part * 4, 4)]
         else:
-            dst = slots.at[pl.ds(source_at(tree, node) * CAP, CAP), rows_of(tree), :]
+            dst = leaf_place(source_at(tree, node), tree, node, part)
         return pltpu.make_async_remote_copy(
             src_ref=dst, dst_ref=dst, send_sem=row_send.at[tree, i, part or 0], recv_sem=row_recv.at[tree, i, part or 0],
             device_id=(pair, coup_at(*DIRS[0])), device_id_type=MESH,
@@ -157,9 +168,9 @@
         while position < upto:
             tree, node, part = ORDER[position]
             if TREE[node] != ROOT:
-                for half in (0, 1) if part is None else (part,):
+                for half in (0, 1) if node in LEAVES else (part,):
                     await_rows(tree, TREE[node], half)
-            if node in LEAVES:
+            if node in LEAVES and part != 1:
                 pack(tree, node)
             start(row_copy(tree, node, part))
             position += 1
@@ -219,7 +230,7 @@
         )
 
     zero = jnp.zeros((1, 128), jnp.int32)
-    wanted, row_of, _, rank = lax.fori_loop(0, TASKS, list_step, (zero, zero, zero, zero), unroll=8)
+    wanted, row_of, _, rank = lax.fori_loop(0, TASKS, list_step, (zero, zero - 1, zero, zero), unroll=8)
     lists[0:1, :] = wanted
     lists[1:2, :] = row_of
     lists[2:3, :] = jnp.maximum(peers, 0) * CAP + rank
@@ -268,23 +279,30 @@
         move.wait()
 
     lax.fori_loop(2, 8, first_part, 0)
+    for n in LAST:
+        for t in (2, 3):
+            slots[coup_at((-n[0]) % SIDE, (-n[1]) % SIDE) * CAP + t] = jnp.zeros((V, V), jnp.bfloat16)
     for t in range(CAP):
         slots[coup * CAP + t] = own[lists_s[0, coup * CAP + t]]
 
     def product(a, b, transposed=False):
         dims = (((1,), (1 if transposed else 0,)), ((), ()))
         return lax.dot_general(a, b, dims, preferred_element_type=jnp.float32)
+
+    def link_of(slot, source):
+        r = lists_s[1, slot]
+        some = jnp.maximum(r, 0)
+        f = fock[source * 2 + lists_s[0, slot] % 2, coup * 2 + (some // LINKS) % 2]
+        return some, jnp.where(r < 0, 0.0, f)
 
     def row_first(*nodes):
         for n in nodes:
             source_ready(n)
         for n in nodes:
             source = coup_at((-n[0]) % SIDE, (-n[1]) % SIDE)
-            for t in range(CAP):
+            for t in range(2 if n in LAST else CAP):
                 slot = source * CAP + t
-                r = lists_s[1, slot]
-                k = source * 2 + lists_s[0, slot] % 2
-                f = fock[k, coup * 2 + (r // LINKS) % 2]
+                r, f = link_of(slot, source)
                 slots[slot] = (f * product(srow[r], slots[slot])).astype(jnp.bfloat16)
 
     def wide(blocks):
@@ -308,7 +326,7 @@
             m = sign(tree, n)
             if m in LEAVES and (tree, m) not in leaf_done:
                 leaf_done.add((tree, m))
-                row_arrival(tree, m, None).wait_recv()
+                row_arrival(tree, m, 0 if m in LAST else None).wait_recv()
 
     for n in ((0, 1), (3, 0)):
         for tree in range(2):
@@ -327,7 +345,7 @@
     row_first((1, 1), (3, 3))
     row_first((1, 0), (3, 0))
     loads[3].wait()
-    send_rows(40)
+    send_rows(44)
     y_copy(1, 0, 1).wait_recv()
     start(c_copy(2, 0))
     y_copy(3, 1, 1).wait_recv()
@@ -348,24 +366,47 @@
     row_id = lax.broadcasted_iota(jnp.int32, (V, 1), 0)
     col_id = lax.broadcasted_iota(jnp.int32, (1, V), 1)
 
-    def last_part(p):
+    def mask_of(p):
+        return (row_id < count[p]).astype(jnp.float32) * (col_id < count[p]).astype(jnp.float32)
+
+    for p in range(BLOCKS):
         rows = [p * LINKS + s for s in range(LINKS)]
-        full = full_part[p] - product(wide([slots[lists_s[2, r]] for r in rows]), wide([srow[r] for r in rows]), True)
-        n = count[p]
-        mask = (row_id < n).astype(jnp.float32) * (col_id < n).astype(jnp.float32)
-        res_v[p] = (mask * full).astype(jnp.bfloat16)
-        new_v[p] = (mask * (own[p].astype(jnp.float32) - full * inv_den[p])).astype(jnp.bfloat16)
-
-    for p in range(BLOCKS):
-        last_part(p)
+        mask = mask_of(p)
+        term = product(wide([slots[lists_s[2, r]] for r in rows]), wide([srow[r] for r in rows]), True)
+        full_part[p] = mask * (full_part[p] - term)
+        own[p] = (mask * own[p].astype(jnp.float32)).astype(jnp.bfloat16)
+
+    for tree in range(2):
+        for n in LAST:
+            await_rows(tree, n, 1)
+    middles = []
+    for u in range(2 * len(LAST)):
+        n = LAST[u // 2]
+        source = coup_at((-n[0]) % SIDE, (-n[1]) % SIDE)
+        r, f = link_of(source * CAP + 2 + u % 2, source)
+        middles.append((r, (f * product(srow[r], late[u])).astype(jnp.bfloat16)))
+    for u, (r, middle) in enumerate(middles):
+        p = r // LINKS
+        late_part[u] = mask_of(p) * product(middle, srow[r], True)
+        late_pair[u : u + 1, :] = jnp.full((1, 128), p, jnp.int32)
+
     for copy in started:
         copy.wait_send()
 
 
-def copy_kernel(a, b, a_out, b_out, sem):
-    stores = [pltpu.make_async_copy(a, a_out, sem.at[0]), pltpu.make_async_copy(b, b_out, sem.at[1])]
-    for store in stores:
-        store.start()
+def results_kernel(own, _, inv_den, late_part, late_pair, res_out, new_out, full_part, res_v, new_v, sem):
+    stores = []
+    pairs = [jnp.max(late_pair[u : u + 1, :]) for u in range(2 * len(LAST))]
+    for u, p in enumerate(pairs):
+        full_part[p] = full_part[p] - late_part[u]
+    for p in range(BLOCKS):
+        full = full_part[p]
+        res_v[p] = full.astype(jnp.bfloat16)
+        new_v[p] = (own[p].astype(jnp.float32) - full * inv_den[p]).astype(jnp.bfloat16)
+        stores.append(pltpu.make_async_copy(res_v.at[p], res_out.at[p], sem.at[0, p]))
+        stores.append(pltpu.make_async_copy(new_v.at[p], new_out.at[p], sem.at[1, p]))
+        stores[-2].start()
+        stores[-1].start()
     for store in stores:
         store.wait()
 
@@ -378,24 +419,25 @@
     bf16, f32, i32 = jnp.bfloat16, jnp.float32, jnp.int32
     dma = pltpu.SemaphoreType.DMA
     block = (BLOCKS, V, V)
-    residual, new = pl.pallas_call(
+    parts = pl.pallas_call(
         kernel,
-        out_shape=(pltpu.VMEM(block, bf16), pltpu.VMEM(block, bf16)),
+        out_shape=(
+            pltpu.VMEM(block, bf16), pltpu.VMEM(block, f32), pltpu.VMEM(block, f32),
+            pltpu.VMEM((2 * len(LAST), V, V), f32), pltpu.VMEM((8, 128), i32),
+        ),
         in_specs=[hbm] * 11,
-        out_specs=(vmem, vmem),
+        out_specs=(vmem,) * 5,
         scratch_shapes=[
             pltpu.SMEM((LINKS, 1, BLOCKS), i32), pltpu.SMEM((BLOCKS, LINKS), i32), pltpu.SMEM((BLOCKS, LINKS), i32),
             pltpu.SMEM((BLOCKS,), i32), pltpu.SMEM((32, 32), f32), pltpu.SMEM((32,), f32), pltpu.VMEM((BLOCKS, V), f32),
-            pltpu.VMEM(block, bf16),
             pltpu.VMEM(block, bf16),
             pltpu.VMEM((TASKS, V, V), bf16),
             pltpu.VMEM((TASKS, V, V), bf16),
             pltpu.VMEM((8 * BLOCKS, V, V), bf16),
             pltpu.VMEM((N_COUP * CAP, V, V), bf16),
+            pltpu.VMEM((2 * len(LAST), V, V), bf16),
             [pltpu.VMEM((BLOCKS, HALF, V), bf16)] * (2 * len(INNER)),
             pltpu.VMEM((2 * len(LEAVES), CAP, HALF, V), bf16),
-            pltpu.VMEM(block, f32),
-            pltpu.VMEM(block, f32),
             pltpu.VMEM((8, 128), i32),
             pltpu.VMEM((4, 8, 128), i32),
             pltpu.SMEM((8, 128), i32),
@@ -404,7 +446,7 @@
             dma((2, len(NODES), 2)), dma((2, len(NODES), 2)), dma((6,)), dma((6,)), dma((8,)), dma((8,)),
         ],
         compiler_params=pltpu.CompilerParams(
-            collective_id=0, has_side_effects=True, vmem_limit_bytes=54 * 2**20
+            collective_id=0, has_side_effects=True, vmem_limit_bytes=52 * 2**20
         ),
         cost_estimate=pl.CostEstimate(flops=96 * 4 * V**3, bytes_accessed=16 * 2**20, transcendentals=0),
         name="residual_iteration",
@@ -414,15 +456,16 @@
         row_intersection.reshape(TASKS, V, V), column_intersection.reshape(TASKS, V, V),
     )
     return pl.pallas_call(
-        copy_kernel,
-        out_shape=(jax.ShapeDtypeStruct(block, bf16), jax.ShapeDtypeStruct(block, bf16)),
-        in_specs=[vmem, vmem],
-        out_specs=(hbm, hbm),
-        scratch_shapes=[dma((2,))],
-        compiler_params=pltpu.CompilerParams(vmem_limit_bytes=54 * 2**20),
+        results_kernel,
+        out_shape=(jax.ShapeDtypeStruct(block, bf16), jax.ShapeDtypeStruct(block, bf16), pltpu.VMEM(block, f32)),
+        input_output_aliases={1: 2},
+        in_specs=[vmem] * 5,
+        out_specs=(hbm, hbm, vmem),
+        scratch_shapes=[pltpu.VMEM(block, bf16), pltpu.VMEM(block, bf16), dma((2, BLOCKS))],
+        compiler_params=pltpu.CompilerParams(vmem_limit_bytes=52 * 2**20),
         cost_estimate=pl.CostEstimate(flops=0, bytes_accessed=4 * 2**20, transcendentals=0),
         name="results",
-    )(*(pltpu.with_memory_space_constraint(a, pltpu.VMEM) for a in (residual, new)))
+    )(*(pltpu.with_memory_space_constraint(a, pltpu.VMEM) for a in parts))[:2]
 
 
 def solution(mesh):

time: 70.7 us -> 69.6 us (0.984)
  Pallas kernels: 69.9 us -> 68.8 us
    pallas_call x1, Pallas kernels: 68.6 us -> 67.1 us  [on_device(): pl.pallas_call(kernel, out_shape=(pltpu.VMEM(block, bf16), pltpu.VMEM(blo...]
where the time goes in v5:
time: 69.6 us; the launch traced here: 69.5 us
  Pallas kernels  68.8 us (99%)
    pallas_call x1, Pallas kernels, on_device(): pl.pallas_call(kernel, out_shape=(pltpu.VMEM(block, bf16), pltpu.VMEM(blo...  67.1 us
    pallas_call x1, Pallas kernels, on_device(): pl.pallas_call(results_kernel, out_shape=(jax.ShapeDtypeStruct(block, bf1...  1.77 us

profile of v5, /device:TPU:0, one launch (start us, length us, event | category | flops | bytes accessed | tf_op | source)
XLA Modules:
  0.0 69.5 jit_solution(1356480436160980924)
XLA Ops:
  0.6 67.1 %residual_iteration.1 = (bf16[8,256,256]{2,1,0:T(8,128)(2,1)S(1)}, f32[8,256,256]{2,1,0:T(8,128)S(1)}, f32[8,256,256]{2,1,0:T(8,128)S(1)}, f32[4,256,256]{2,1,0:T(8,128)S(1)}, s32[8,128]{1,0:T(8,128)S(1)}) custom-call(s32[6,1,8]{2,1,0:T(1,128)} %bitcast.5, s32[8,6]{1,0:T(8,128)} %offset_h.1, s32[8,6]{1,0:T(8,128)} %partner_h.1, s32[8]{0:T(128)} %count_h.1, ...), custom_call_target="tpu_custom_call" | custom-call | flops 6442450944 | bytes 16777216 | tf_op jit(solution)/shard_map/residual_iteration/pallas_call | solution.py:422
  67.7 1.8 %results.1 = (bf16[8,256,256]{2,1,0:T(8,128)(2,1)}, bf16[8,256,256]{2,1,0:T(8,128)(2,1)}, f32[8,256,256]{2,1,0:T(8,128)S(1)}) custom-call(bf16[8,256,256]{2,1,0:T(8,128)(2,1)S(1)} %get-tuple-element.9.own, f32[8,256,256]{2,1,0:T(8,128)S(1)} %get-tuple-element.10._, f32[8,256,256]{2,1,0:T(8,128)S(1)} %get-tuple-element.11.inv_den, ...), custom_call_target="tpu_custom_call", output_to_operand_aliasing={{2}: (1, {})} | custom-call | bytes 4194304 | tf_op jit(solution)/shard_map/results/pallas_call | solution.py:458

commit v6 on v5

--- a/solution.py
+++ b/solution.py
@@ -39,7 +39,10 @@
 LAST = [(0, 2), (2, 2)]
 INNER = [n for n in TREE if n in TREE.values()]
 LEAVES = [n for n in TREE if n not in TREE.values()]
-NODES = INNER + LEAVES
+GROUPS = {}
+for _i, _copy in enumerate(ORDER):
+    GROUPS.setdefault((_i // 4, _copy[1] in LEAVES), []).append(_copy)
+GROUPS = list(GROUPS.values())
 DIRS = [(1, 0), (3, 0), (0, 1), (0, 3)]
 
 
@@ -53,7 +56,7 @@
     peer, offset, partner, count, fock, occ, energy,
     k_in, srow, scol, cols, slots, late, inner, packed,
     lists, lists_in, lists_s, lists_in_s,
-    small_sem, in_sem, list_send, list_recv, list_local, row_send, row_recv, y_send, y_recv, c_send, c_recv,
+    small_sem, in_sem, list_send, list_recv, list_local, row_send, row_recv, col_send, y_recv, c_recv,
 ):
     pair, coup = lax.axis_index("pair"), lax.axis_index("coup")
     y, core = pair // 2, pair % 2
@@ -104,9 +107,9 @@
             if part is not None:
                 src = src.at[pl.ds(part * 2, 2)]
             dst = leaf_place(source, tree, node, part)
-        i = NODES.index(node)
+        group = [(tree, node, part) in g for g in GROUPS].index(True)
         return pltpu.make_async_remote_copy(
-            src_ref=src, dst_ref=dst, send_sem=row_send.at[tree, i, part or 0], recv_sem=row_recv.at[tree, i, part or 0],
+            src_ref=src, dst_ref=dst, send_sem=row_send.at[tree], recv_sem=row_recv.at[group],
             device_id=(pair, coup_at(*step)), device_id_type=MESH,
         )
 
@@ -117,16 +120,8 @@
     def inner_of(tree, node):
         return inner[tree * len(INNER) + INNER.index(node)]
 
-    def row_arrival(tree, node, part):
-        i = NODES.index(node)
-        if node in INNER:
-            dst = inner_of(tree, node).at[pl.ds(part * 4, 4)]
-        else:
-            dst = leaf_place(source_at(tree, node), tree, node, part)
-        return pltpu.make_async_remote_copy(
-            src_ref=dst, dst_ref=dst, send_sem=row_send.at[tree, i, part or 0], recv_sem=row_recv.at[tree, i, part or 0],
-            device_id=(pair, coup_at(*DIRS[0])), device_id_type=MESH,
-        )
+    def take(ref, semaphore):
+        pltpu.make_async_copy(ref, ref, semaphore).wait()
 
     def col_region(source, part):
         return cols.at[pl.ds(source * BLOCKS + part * 4, 4)]
@@ -136,32 +131,30 @@
         src = amp.at[pl.ds(part * 4, 4)] if hop == 0 else col_region(source, part)
         i = (0 if dy == 1 else 3) + (part if hop == 0 else 2)
         return pltpu.make_async_remote_copy(
-            src_ref=src, dst_ref=col_region(source, part), send_sem=y_send.at[i], recv_sem=y_recv.at[i],
+            src_ref=src, dst_ref=col_region(source, part), send_sem=col_send.at[0], recv_sem=y_recv.at[i],
             device_id=(pair_at(dy), coup), device_id_type=MESH,
         )
 
     def c_copy(dy, part):
-        i = dy * 2 + part
         source = pair_at(dy)
         src = amp.at[pl.ds(part * 4, 4)] if dy == 0 else col_region(source, part)
         return pltpu.make_async_remote_copy(
-            src_ref=src, dst_ref=col_region(source, part), send_sem=c_send.at[i], recv_sem=c_recv.at[i],
+            src_ref=src, dst_ref=col_region(source, part), send_sem=col_send.at[0], recv_sem=c_recv.at[0],
             device_id=(pair_at(0, 1), coup), device_id_type=MESH,
         )
 
-    started = []
-
     def start(copy):
         copy.start()
-        started.append(copy)
 
     position = 0
     arrived = set()
 
     def await_rows(tree, node, part):
-        if (tree, node, part) not in arrived:
-            arrived.add((tree, node, part))
-            row_arrival(tree, node, part).wait_recv()
+        group = [(tree, node, part) in g for g in GROUPS].index(True)
+        if group not in arrived:
+            arrived.add(group)
+            halves = sum(2 if n in LAST else 4 for _, n, _ in GROUPS[group])
+            take(packed.at[pl.ds(0, halves // 4)], row_recv.at[group])
 
     def send_rows(upto):
         nonlocal position
@@ -237,13 +230,13 @@
 
     def list_copy(i):
         return pltpu.make_async_remote_copy(
-            src_ref=lists, dst_ref=lists_in.at[i], send_sem=list_send.at[i], recv_sem=list_recv.at[i],
+            src_ref=lists, dst_ref=lists_in.at[i], send_sem=list_send.at[0], recv_sem=list_recv.at[0],
             device_id=(pair, coup_at((-DIRS[i][0]) % SIDE, (-DIRS[i][1]) % SIDE)), device_id_type=MESH,
         )
 
     for i in range(4):
         start(list_copy(i))
-    to_scalars = pltpu.make_async_copy(lists, lists_s, list_local.at[4])
+    to_scalars = pltpu.make_async_copy(lists, lists_s, list_local.at[1])
     to_scalars.start()
 
     send_rows(12)
@@ -270,13 +263,10 @@
     start(y_copy(3, 1, 1))
     start(c_copy(1, 1))
     to_scalars.wait()
-    moves = []
-    for i in range(4):
-        list_copy(i).wait_recv()
-        moves.append(pltpu.make_async_copy(lists_in.at[i], lists_in_s.at[i], list_local.at[i]))
-        moves[-1].start()
-    for move in moves:
-        move.wait()
+    take(lists_in, list_recv.at[0])
+    move = pltpu.make_async_copy(lists_in, lists_in_s, list_local.at[0])
+    move.start()
+    move.wait()
 
     lax.fori_loop(2, 8, first_part, 0)
     for n in LAST:
@@ -319,14 +309,11 @@
         full_part[p] = full_part[p] - product(wide(parts), wide(intersections), True)
         return 0
 
-    leaf_done = set()
-
     def source_ready(n):
         for tree in range(2):
             m = sign(tree, n)
-            if m in LEAVES and (tree, m) not in leaf_done:
-                leaf_done.add((tree, m))
-                row_arrival(tree, m, 0 if m in LAST else None).wait_recv()
+            if m in LEAVES:
+                await_rows(tree, m, 0 if m in LAST else None)
 
     for n in ((0, 1), (3, 0)):
         for tree in range(2):
@@ -353,9 +340,7 @@
     for tree in range(2):
         keep(tree, (1, 2))
     row_first((2, 0))
-    for dy in range(4):
-        for part in range(2):
-            c_copy(dy, part).wait_recv()
+    take(cols.at[pl.ds(0, 4 * BLOCKS)], c_recv.at[0])
     lax.fori_loop(0, 3, col_pair, 0)
     row_first((0, 1), (0, 3))
     lax.fori_loop(3, 8, col_pair, 0)
@@ -390,8 +375,10 @@
         late_part[u] = mask_of(p) * product(middle, srow[r], True)
         late_pair[u : u + 1, :] = jnp.full((1, 128), p, jnp.int32)
 
-    for copy in started:
-        copy.wait_send()
+    take(lists_in, list_send.at[0])
+    take(cols.at[pl.ds(0, 7 * BLOCKS)], col_send.at[0])
+    for tree in range(2):
+        take(packed, row_send.at[tree])
 
 
 def results_kernel(own, _, inv_den, late_part, late_pair, res_out, new_out, full_part, res_v, new_v, sem):
@@ -442,8 +429,8 @@
             pltpu.VMEM((4, 8, 128), i32),
             pltpu.SMEM((8, 128), i32),
             pltpu.SMEM((4, 8, 128), i32),
-            dma((7,)), dma((5,)), dma((4,)), dma((4,)), dma((5,)),
-            dma((2, len(NODES), 2)), dma((2, len(NODES), 2)), dma((6,)), dma((6,)), dma((8,)), dma((8,)),
+            dma((7,)), dma((5,)), dma((1,)), dma((1,)), dma((2,)), dma((2,)), dma((len(GROUPS),)), dma((1,)), dma((6,)),
+            dma((1,)),
         ],
         compiler_params=pltpu.CompilerParams(
             collective_id=0, has_side_effects=True, vmem_limit_bytes=52 * 2**20

time: 69.6 us -> 68.3 us (0.981)
  Pallas kernels: 68.8 us -> 67.5 us
    pallas_call x1, Pallas kernels: 67.1 us -> 65.8 us  [on_device(): pl.pallas_call(kernel, out_shape=(pltpu.VMEM(block, bf16), pltpu.VMEM(blo...]
where the time goes in v6:
time: 68.3 us; the launch traced here: 68.2 us
  Pallas kernels  67.5 us (99%)
    pallas_call x1, Pallas kernels, on_device(): pl.pallas_call(kernel, out_shape=(pltpu.VMEM(block, bf16), pltpu.VMEM(blo...  65.8 us
    pallas_call x1, Pallas kernels, on_device(): pl.pallas_call(results_kernel, out_shape=(jax.ShapeDtypeStruct(block, bf1...  1.77 us

profile of v6, /device:TPU:0, one launch (start us, length us, event | category | flops | bytes accessed | tf_op | source)
XLA Modules:
  0.0 68.2 jit_solution(18062212061895291800)
XLA Ops:
  0.6 65.8 %residual_iteration.1 = (bf16[8,256,256]{2,1,0:T(8,128)(2,1)S(1)}, f32[8,256,256]{2,1,0:T(8,128)S(1)}, f32[8,256,256]{2,1,0:T(8,128)S(1)}, f32[4,256,256]{2,1,0:T(8,128)S(1)}, s32[8,128]{1,0:T(8,128)S(1)}) custom-call(s32[6,1,8]{2,1,0:T(1,128)} %bitcast.5, s32[8,6]{1,0:T(8,128)} %offset_h.1, s32[8,6]{1,0:T(8,128)} %partner_h.1, s32[8]{0:T(128)} %count_h.1, ...), custom_call_target="tpu_custom_call" | custom-call | flops 6442450944 | bytes 16777216 | tf_op jit(solution)/shard_map/residual_iteration/pallas_call | solution.py:409
  66.4 1.8 %results.1 = (bf16[8,256,256]{2,1,0:T(8,128)(2,1)}, bf16[8,256,256]{2,1,0:T(8,128)(2,1)}, f32[8,256,256]{2,1,0:T(8,128)S(1)}) custom-call(bf16[8,256,256]{2,1,0:T(8,128)(2,1)S(1)} %get-tuple-element.9.own, f32[8,256,256]{2,1,0:T(8,128)S(1)} %get-tuple-element.10._, f32[8,256,256]{2,1,0:T(8,128)S(1)} %get-tuple-element.11.inv_den, ...), custom_call_target="tpu_custom_call", output_to_operand_aliasing={{2}: (1, {})} | custom-call | bytes 4194304 | tf_op jit(solution)/shard_map/results/pallas_call | solution.py:445

commit v7 on v6

--- a/solution.py
+++ b/solution.py
@@ -74,7 +74,7 @@
     ]
     large = [(amp, own), (amp, cols.at[pl.ds(pair * BLOCKS, BLOCKS)]), (integ, k_in), (s_col, scol), (s_row, srow)]
     small_loads = [pltpu.make_async_copy(a, b, small_sem.at[i]) for i, (a, b) in enumerate(small)]
-    loads = [pltpu.make_async_copy(a, b, in_sem.at[i]) for i, (a, b) in enumerate(large)]
+    loads = [pltpu.make_async_copy(a, b, in_sem.at[max(i - 2, 0)]) for i, (a, b) in enumerate(large)]
 
     barrier = pltpu.get_barrier_semaphore()
     friends = [(pair, coup_at(*d)) for d in DIRS] + [(pair_at(d), coup) for d in (1, 3)] + [(pair_at(0, 1), coup)]
@@ -241,8 +241,7 @@
 
     send_rows(12)
 
-    for load in loads[:3]:
-        load.wait()
+    take(cols.at[pl.ds(0, 3 * BLOCKS)], in_sem.at[0])
 
     def first_part(p, _):
         e = energy[pl.ds(p, 1), :]
@@ -382,7 +381,6 @@
 
 
 def results_kernel(own, _, inv_den, late_part, late_pair, res_out, new_out, full_part, res_v, new_v, sem):
-    stores = []
     pairs = [jnp.max(late_pair[u : u + 1, :]) for u in range(2 * len(LAST))]
     for u, p in enumerate(pairs):
         full_part[p] = full_part[p] - late_part[u]
@@ -390,12 +388,12 @@
         full = full_part[p]
         res_v[p] = full.astype(jnp.bfloat16)
         new_v[p] = (own[p].astype(jnp.float32) - full * inv_den[p]).astype(jnp.bfloat16)
-        stores.append(pltpu.make_async_copy(res_v.at[p], res_out.at[p], sem.at[0, p]))
-        stores.append(pltpu.make_async_copy(new_v.at[p], new_out.at[p], sem.at[1, p]))
-        stores[-2].start()
-        stores[-1].start()
-    for store in stores:
-        store.wait()
+        if p % 2 == 1:
+            two = pl.ds(p - 1, 2)
+            pltpu.make_async_copy(res_v.at[two], res_out.at[two], sem.at[0]).start()
+            pltpu.make_async_copy(new_v.at[two], new_out.at[two], sem.at[1]).start()
+    pltpu.make_async_copy(res_v, res_out, sem.at[0]).wait()
+    pltpu.make_async_copy(new_v, new_out, sem.at[1]).wait()
 
 
 def on_device(
@@ -429,7 +427,7 @@
             pltpu.VMEM((4, 8, 128), i32),
             pltpu.SMEM((8, 128), i32),
             pltpu.SMEM((4, 8, 128), i32),
-            dma((7,)), dma((5,)), dma((1,)), dma((1,)), dma((2,)), dma((2,)), dma((len(GROUPS),)), dma((1,)), dma((6,)),
+            dma((7,)), dma((3,)), dma((1,)), dma((1,)), dma((2,)), dma((2,)), dma((len(GROUPS),)), dma((1,)), dma((6,)),
             dma((1,)),
         ],
         compiler_params=pltpu.CompilerParams(
@@ -448,7 +446,7 @@
         input_output_aliases={1: 2},
         in_specs=[vmem] * 5,
         out_specs=(hbm, hbm, vmem),
-        scratch_shapes=[pltpu.VMEM(block, bf16), pltpu.VMEM(block, bf16), dma((2, BLOCKS))],
+        scratch_shapes=[pltpu.VMEM(block, bf16), pltpu.VMEM(block, bf16), dma((2,))],
         compiler_params=pltpu.CompilerParams(vmem_limit_bytes=52 * 2**20),
         cost_estimate=pl.CostEstimate(flops=0, bytes_accessed=4 * 2**20, transcendentals=0),
         name="results",

time: 68.3 us -> 68.2 us (level)
  no operation moved by 1% of the time
where the time goes in v7:
time: 68.2 us; the launch traced here: 68.1 us
  Pallas kernels  67.4 us (99%)
    pallas_call x1, Pallas kernels, on_device(): pl.pallas_call(kernel, out_shape=(pltpu.VMEM(block, bf16), pltpu.VMEM(blo...  65.7 us
    pallas_call x1, Pallas kernels, on_device(): pl.pallas_call(results_kernel, out_shape=(jax.ShapeDtypeStruct(block, bf1...  1.7 us

profile of v7, /device:TPU:0, one launch (start us, length us, event | category | flops | bytes accessed | tf_op | source)
XLA Modules:
  0.0 68.1 jit_solution(10689912422222301064)
XLA Ops:
  0.6 65.7 %residual_iteration.1 = (bf16[8,256,256]{2,1,0:T(8,128)(2,1)S(1)}, f32[8,256,256]{2,1,0:T(8,128)S(1)}, f32[8,256,256]{2,1,0:T(8,128)S(1)}, f32[4,256,256]{2,1,0:T(8,128)S(1)}, s32[8,128]{1,0:T(8,128)S(1)}) custom-call(s32[6,1,8]{2,1,0:T(1,128)} %bitcast.5, s32[8,6]{1,0:T(8,128)} %offset_h.1, s32[8,6]{1,0:T(8,128)} %partner_h.1, s32[8]{0:T(128)} %count_h.1, ...), custom_call_target="tpu_custom_call" | custom-call | flops 6442450944 | bytes 16777216 | tf_op jit(solution)/shard_map/residual_iteration/pallas_call | solution.py:407
  66.4 1.7 %results.1 = (bf16[8,256,256]{2,1,0:T(8,128)(2,1)}, bf16[8,256,256]{2,1,0:T(8,128)(2,1)}, f32[8,256,256]{2,1,0:T(8,128)S(1)}) custom-call(bf16[8,256,256]{2,1,0:T(8,128)(2,1)S(1)} %get-tuple-element.9.own, f32[8,256,256]{2,1,0:T(8,128)S(1)} %get-tuple-element.10._, f32[8,256,256]{2,1,0:T(8,128)S(1)} %get-tuple-element.11.inv_den, ...), custom_call_target="tpu_custom_call", output_to_operand_aliasing={{2}: (1, {})} | custom-call | bytes 4194304 | tf_op jit(solution)/shard_map/results/pallas_call | solution.py:443
